TPU v7x, 256 devices: a whole 4x4x8 slice. The times are simulated.
256 devices in a mesh: grp: 16 (over x, y), col: 16 (over z, core).
Axes of the slice: x: 4, y: 4, z: 8, core: 2. Of those that a mesh axis runs over, the one named last changes fastest.
Arguments:
- features: bfloat16 [128, 1048576], P('col', 'grp'), may hold values from -6 to 6
- adj_tiles: bfloat16 [4096, 128, 128], P('grp'), may hold values from -0.125 to 0.125
- tile_dst: int32 [4096], P('grp'), may hold values from 0 to 15
- tile_src: int32 [4096], P('grp'), may hold values from 0 to 8191, as said below
- dst_ids: int32 [256], P('grp'), may hold values from 0 to 8191, as said below
- self_coef: float32 [32768], P('grp'), may hold values from 0.2 to 2
- weight: bfloat16 [128, 128], replicated, may hold values from -0.5 to 0.5
- out_bias: float32 [128], replicated, may hold values from -3 to 3
Outputs:
- layer_out: bfloat16 [32768, 128], P(('grp', 'col'))
Inputs may be any that keep to these rules, and one draw needn't show every extreme that they name: `tile_src`: tiles of group k name, of every other group, exactly 4 distinct source blocks; the rest name blocks of group k. `dst_ids`: the destination blocks of group k are distinct blocks stored in group k.
All inputs are finite; a program needn't handle non-finite values.
Results may differ from a plain program's by a relative error of at most 0.0047.
Values may be sent and summed in bfloat16 or wider, within the bound.
No kernel may reach another device: no remote copies, remote signals or barrier semaphores. Data moves between devices by JAX's collectives and lax.ppermute only.
A program may use at most 64 MiB of HBM per device.

v0:
```python
import jax
import jax.numpy as jnp
from jax import lax
from jax.sharding import PartitionSpec as P


def per_device(features, adj_tiles, tile_dst, tile_src, dst_ids, self_coef, weight, out_bias):
    feat_cols = features.shape[0]
    block_len = adj_tiles.shape[1]
    group_len = features.shape[1] // block_len
    dst_count = dst_ids.shape[0]
    group_count = lax.axis_size("grp")
    group_index = lax.axis_index("grp")
    own_blocks = features.reshape(feat_cols, group_len, block_len)
    local_dst = dst_ids - group_index * group_len
    self_feats = jnp.take(own_blocks, local_dst, axis=1).astype(jnp.float32).transpose(1, 0, 2)
    source_table = lax.all_gather(features, "grp", axis=1, tiled=True)
    source_table = source_table.reshape(feat_cols, group_count * group_len, block_len)
    picked = jnp.take(source_table, tile_src, axis=1)
    products = jnp.einsum("ftj,tij->tfi", picked, adj_tiles, preferred_element_type=jnp.float32)
    onehot = (tile_dst[None, :] == jnp.arange(dst_count, dtype=jnp.int32)[:, None]).astype(
        jnp.float32
    )
    summed = jnp.einsum("dt,tfi->dfi", onehot, products, precision=lax.Precision.HIGHEST)
    coefs = self_coef.reshape(dst_count, 1, block_len)
    aggregated = (summed + coefs * self_feats).astype(jnp.bfloat16)
    row_layout = lax.all_to_all(aggregated, "col", split_axis=0, concat_axis=1, tiled=True)
    mixed = (
        jnp.einsum("dfi,fo->dio", row_layout, weight, preferred_element_type=jnp.float32) + out_bias
    )
    result = jax.nn.relu(mixed).astype(jnp.bfloat16)
    return result.reshape(row_layout.shape[0] * block_len, weight.shape[1])


def solution(mesh):
    in_specs = (
        P("col", "grp"),
        P("grp", None, None),
        P("grp"),
        P("grp"),
        P("grp"),
        P("grp"),
        P(),
        P(),
    )
    out_specs = P(("grp", "col"), None)
    return jax.shard_map(
        per_device, mesh=mesh, in_specs=in_specs, out_specs=out_specs, check_vma=False
    )
```

profile of v0, /device:TPU:1, one launch (start us, length us, event | category | flops | bytes accessed | tf_op | source)
XLA Modules:
  0.0 166.5 jit_solution(10856082587089450082)
XLA Ops:
  6.5 0.0 copy-start
  6.5 0.0 copy-start.1
  6.5 0.0 copy-start.2
  6.5 0.0 copy-start.3
  6.5 0.0 all-gather.2.cloned.1.call-start
  6.6 0.7 all-gather.2.cloned.1.call-update
  7.3 0.7 compare_and_fusion
  8.0 1.8 %gather_fusion.1 = bf16[16,8,128]{2,1,0:T(8,128)(2,1)S(1)} fusion(bf16[8,512,128]{2,0,1:T(8,128)(2,1)} %bitcast.14, s32[1024]{0:T(1024)S(1)} %pad_clamp_fusion), kind=kCustom, calls=%fused_computation.1 | custom fusion | bytes 65600 | tf_op jit(solution)/shard_map/jit(_take)/gather | solution.py:16
  9.8 0.7 compare_select_fusion
  10.4 0.7 compare_and_fusion.1
  11.1 118.8 %all-gather.2.cloned.1.call-done = bf16[8,1048576]{1,0:T(8,128)(2,1)} async-done(((bf16[8,65536]{1,0:T(8,128)(2,1)}), bf16[8,1048576]{1,0:T(8,128)(2,1)}) %all-gather.2.cloned.1.call-update) | async-done | bytes 16777232 | tf_op jit(solution)/shard_map/all_gather | solution.py:17
  129.9 6.6 %gather_fusion = bf16[256,8,128]{2,1,0:T(8,128)(2,1)S(1)} fusion(bf16[8,8192,128]{2,0,1:T(8,128)(2,1)} %bitcast.15, s32[1024]{0:T(1024)S(1)} %pad_clamp_fusion.1), kind=kCustom, calls=%fused_computation | custom fusion | bytes 1049600 | tf_op jit(solution)/shard_map/jit(_take)/gather | solution.py:19
  136.5 6.8 %fusion.4 = f32[256,8,128]{2,1,0:T(8,128)S(1)} fusion(bf16[256,128,128]{2,1,0:T(8,128)(2,1)} %param.9, bf16[256,8,128]{2,1,0:T(8,128)(2,1)S(1)} %gather_fusion, pred[256]{0:T(512)(128)(4,1)S(1)} %compare_and_fusion.1), kind=kOutput, calls=%fused_computation.8 | convolution fusion | flops 67371008 | bytes 9961728 | tf_op jit(solution)/shard_map/ftj,tij->tfi/dot_general | solution.py:20
  143.4 0.0 copy-done.1
  143.4 0.0 copy-done.2
  143.4 0.6 fusion.1
  143.9 14.9 %all_to_all.4 = bf16[16,8,128]{2,1,0:T(8,128)(2,1)S(1)} all-to-all(bf16[16,8,128]{2,1,0:T(8,128)(2,1)S(1)} %copy.13), channel_id=1, replica_groups=mesh['grp'=16,'col'=16] {'col'}, dimensions={0} | all-to-all | bytes 65536 | tf_op jit(solution)/shard_map/all_to_all | solution.py:27
  158.9 0.0 copy-done
  158.9 0.0 copy-done.3
  158.9 0.8 fusion.2
  (3 shorter events, 0.0 us)
Async XLA Ops:
  6.5 152.3 %copy-start = (bf16[128,128]{1,0:T(8,128)(2,1)S(1)}, bf16[128,128]{1,0:T(8,128)(2,1)}, u32[]{:S(2)}) copy-start(bf16[128,128]{1,0:T(8,128)(2,1)} %param.14) | copy-start | bytes 98308
  6.5 136.8 %copy-start.1 = (f32[2048]{0:T(1024)S(1)}, f32[2048]{0:T(1024)}, u32[]{:S(2)}) copy-start(f32[2048]{0:T(1024)} %param.13) | copy-start | bytes 24580
  6.5 136.8 %copy-start.2 = (s32[256]{0:T(256)S(1)}, s32[256]{0:T(256)}, u32[]{:S(2)}) copy-start(s32[256]{0:T(256)} %param.10) | copy-start | bytes 3076
  6.5 152.3 %copy-start.3 = (f32[128]{0:T(128)S(1)}, f32[128]{0:T(128)}, u32[]{:S(2)}) copy-start(f32[128]{0:T(128)} %param.15) | copy-start | bytes 1540
  6.5 123.4 %all-gather.2.cloned.1.call-start = ((), (), s32[]{:S(2)}) async-start(), calls=%async_computation.1 | async-start | bytes 17825792 | tf_op jit(solution)/shard_map/all_gather | solution.py:17
Sparse Core Ops, SparseCore 0:
  9.8 120.0 all-gather.1
where the time goes:
time: 167 us
  waiting for transfers between devices  119 us (71%)
  blocking collectives  14.9 us (9%)
  between operations  13.4 us (8%)
  local copies, waits for them, and re-layouts  8.42 us (5%)
  matrix products  8.17 us (5%)
  other arithmetic  2.04 us (1%)
    all_gather x1, waiting for transfers between devices, per_device(): source_table = lax.all_gather(features, 'grp', axis=1, tiled=True)  119 us
    all_to_all x1, blocking collectives, per_device(): lax.all_to_all(aggregated, 'col', split_axis=0, concat_axis=1, tiled=True)  14.9 us
    dot_general x1, matrix products, per_device(): jnp.einsum('ftj,tij->tfi', picked, adj_tiles, preferred_element_type=jnp....  6.81 us
    gather x1, local copies, waits for them, and re-layouts, per_device(): picked = jnp.take(source_table, tile_src, axis=1)  6.59 us
  transfers between devices with their start and end apart: 1, of which 1 were waited for; matrix products, arithmetic and copies ran while one was open for 2% of the time, Pallas kernels for 0%

commit v1 on v0

v1 whole, which is shorter than its diff:
```python
import jax
import jax.numpy as jnp
from jax import lax
from jax.experimental import pallas as pl
from jax.experimental.pallas import tpu as pltpu
from jax.sharding import PartitionSpec as P

NEED = 4
BATCH = 16
BIG = 1 << 30

VMEM = pl.BlockSpec(memory_space=pltpu.VMEM)
SMEM = pl.BlockSpec(memory_space=pltpu.SMEM)


def four_least(values):
    least = []
    for _ in range(NEED):
        low = jnp.min(values, axis=1, keepdims=True)
        least.append(low)
        values = jnp.where(values > low, values, BIG)
    return least


def tile_products(entries, count, load_x, adj_ref, acc_ref):
    zero = jnp.zeros((8, 128), jnp.float32)

    def one_pass(step, carry):
        results = []
        for quad in range(BATCH // 4):
            tiles, xs, dsts = [], [], []
            for q in range(4):
                entry = entries[step * BATCH + quad * 4 + q]
                tiles.append(adj_ref[entry & 255])
                xs.append(load_x(entry >> 13))
                dsts.append((entry >> 8) & 31)
            left = jnp.concatenate([xs[0], zero, xs[2], zero], axis=0)
            right = jnp.concatenate([zero, xs[1], zero, xs[3]], axis=0)
            lhs = jnp.concatenate([left, right], axis=1).astype(jnp.bfloat16)
            rhs = jnp.concatenate(
                [
                    jnp.concatenate([tiles[0], tiles[1]], axis=1),
                    jnp.concatenate([tiles[2], tiles[3]], axis=1),
                ],
                axis=0,
            )
            out = lax.dot_general(
                lhs, rhs, (((1,), (1,)), ((), ())), preferred_element_type=jnp.float32
            )
            results += [
                (dsts[0], out[0:8, 0:128]),
                (dsts[1], out[8:16, 0:128]),
                (dsts[2], out[16:24, 128:256]),
                (dsts[3], out[24:32, 128:256]),
            ]
        for dst, value in results:
            acc_ref[dst] += value
        return carry

    lax.fori_loop(0, (count + BATCH - 1) // BATCH, one_pass, 0)


def local_kernel(
    src_s, dst_s, ids_s, src_v, coef_ref, feat_ref, adj_ref,
    acc_ref, remote_s, counts_s,
    local_s, slot_v, slot_s, sem,
):
    n_tiles = src_s.shape[0]
    group = lax.axis_index("grp")
    group_len = feat_ref.shape[1] // 128
    n_dst = ids_s.shape[0]
    n_grp = lax.axis_size("grp")
    shift = group_len.bit_length() - 1
    src = jnp.broadcast_to(src_v[...], (n_grp, n_tiles))
    mine = (src >> shift) == lax.broadcasted_iota(jnp.int32, (n_grp, n_tiles), 0)
    least = four_least(jnp.where(mine, src, BIG))
    rank = jnp.zeros((n_grp, n_tiles), jnp.int32)
    for low in least[: NEED - 1]:
        rank += jnp.where(mine & (src > low), 1, 0)
    slot_v[...] = (src_v[...] >> shift) * NEED + jnp.sum(rank, axis=0, keepdims=True)
    copy = pltpu.make_async_copy(slot_v, slot_s, sem)
    copy.start()
    for d in range(n_dst):
        place = pl.multiple_of((ids_s[d] - group * group_len) * 128, 128)
        own = feat_ref[:, pl.ds(place, 128)].astype(jnp.float32)
        acc_ref[d] = coef_ref[d : d + 1, :] * own
    acc_ref[n_dst] = jnp.zeros((8, 128), jnp.float32)
    copy.wait()

    def sort_out(t, carry):
        n_local, n_remote = carry
        source = src_s[t]
        head = t + dst_s[t] * 256
        is_local = jnp.where((source >> shift) == group, 1, 0)
        local_s[n_local] = head + (source & (group_len - 1)) * 8192
        remote_s[n_remote] = head + slot_s[0, t] * 8192
        return n_local + is_local, n_remote + 1 - is_local

    n_local, n_remote = lax.fori_loop(0, n_tiles, sort_out, (0, 0), unroll=8)
    for i in range(BATCH):
        local_s[n_local + i] = n_dst * 256
        remote_s[n_remote + i] = n_dst * 256
    counts_s[0] = n_remote

    def load_x(place):
        return feat_ref[:, pl.ds(pl.multiple_of(place * 128, 128), 128)].astype(jnp.float32)

    tile_products(local_s, n_local, load_x, adj_ref, acc_ref)


def gather_kernel(req_ref, feat_ref, out_ref, place_v, place_s, sem):
    group = lax.axis_index("grp")
    group_len = feat_ref.shape[1] // 128
    shift = group_len.bit_length() - 1
    n_grp, n_tiles = req_ref.shape
    req = req_ref[...]
    least = four_least(jnp.where((req >> shift) == group, req & (group_len - 1), BIG))
    lane = lax.broadcasted_iota(jnp.int32, (n_grp, 128), 1)
    table = jnp.zeros((n_grp, 128), jnp.int32)
    for r, low in enumerate(least):
        table = jnp.where(lane == r, jnp.minimum(low, group_len - 1), table)
    place_v[...] = table
    copy = pltpu.make_async_copy(place_v, place_s, sem)
    copy.start()
    copy.wait()
    for k in range(n_grp):
        for r in range(NEED):
            place = pl.multiple_of(place_s[k, r] * 128, 128)
            out_ref[k, r] = feat_ref[:, pl.ds(place, 128)]


def remote_kernel(remote_s, counts_s, recv_ref, acc_in_ref, adj_ref, out_ref, acc_ref, x_ref):
    acc_ref[...] = acc_in_ref[...]
    x_ref[...] = recv_ref[...].astype(jnp.float32)

    def load_x(slot):
        return x_ref[slot]

    tile_products(remote_s, counts_s[0], load_x, adj_ref, acc_ref)
    out_ref[...] = acc_ref[: out_ref.shape[0]].astype(out_ref.dtype)


def per_device(features, adj_tiles, tile_dst, tile_src, dst_ids, self_coef, weight, out_bias):
    n_feat = features.shape[0]
    n_tiles = tile_src.shape[0]
    n_dst = dst_ids.shape[0]
    n_grp = lax.axis_size("grp")
    n_slots = n_grp * NEED
    params = pltpu.CompilerParams(vmem_limit_bytes=32 << 20)
    requests = lax.all_to_all(
        jnp.broadcast_to(tile_src, (n_grp, n_tiles)), "grp", 0, 0, tiled=True
    )
    acc, remote, counts = pl.pallas_call(
        local_kernel,
        name="local",
        out_shape=(
            jax.ShapeDtypeStruct((n_dst + 1, n_feat, 128), jnp.float32),
            jax.ShapeDtypeStruct((n_tiles + BATCH,), jnp.int32),
            jax.ShapeDtypeStruct((1,), jnp.int32),
        ),
        in_specs=[SMEM, SMEM, SMEM, VMEM, VMEM, VMEM, VMEM],
        out_specs=(VMEM, SMEM, SMEM),
        scratch_shapes=[
            pltpu.SMEM((n_tiles + BATCH,), jnp.int32),
            pltpu.VMEM((1, n_tiles), jnp.int32),
            pltpu.SMEM((1, n_tiles), jnp.int32),
            pltpu.SemaphoreType.DMA,
        ],
        compiler_params=params,
        cost_estimate=pl.CostEstimate(
            flops=2 * n_tiles * 128 * 128 * 32, bytes_accessed=9 << 20, transcendentals=0
        ),
    )(
        tile_src, tile_dst, dst_ids, tile_src.reshape(1, n_tiles),
        self_coef.reshape(n_dst, 128), features, adj_tiles,
    )
    blocks = pl.pallas_call(
        gather_kernel,
        name="gather",
        out_shape=jax.ShapeDtypeStruct((n_grp, NEED, n_feat, 128), features.dtype),
        in_specs=[VMEM, VMEM],
        out_specs=VMEM,
        scratch_shapes=[
            pltpu.VMEM((n_grp, 128), jnp.int32),
            pltpu.SMEM((n_grp, 128), jnp.int32),
            pltpu.SemaphoreType.DMA,
        ],
        compiler_params=params,
    )(requests, features)
    arrived = lax.all_to_all(blocks, "grp", 0, 0, tiled=True).reshape(n_slots, n_feat, 128)
    aggregated = pl.pallas_call(
        remote_kernel,
        name="remote",
        out_shape=jax.ShapeDtypeStruct((n_dst, n_feat, 128), jnp.bfloat16),
        in_specs=[SMEM, SMEM, VMEM, VMEM, VMEM],
        out_specs=VMEM,
        scratch_shapes=[
            pltpu.VMEM((n_dst + 1, n_feat, 128), jnp.float32),
            pltpu.VMEM((n_slots, n_feat, 128), jnp.float32),
        ],
        compiler_params=params,
    )(remote, counts, arrived, acc, adj_tiles)
    rows = lax.all_to_all(aggregated, "col", 0, 0, tiled=True).reshape(-1, 128)
    mixed = (
        lax.dot_general(
            rows, weight, (((0,), (0,)), ((), ())), preferred_element_type=jnp.float32
        )
        + out_bias
    )
    return jax.nn.relu(mixed).astype(jnp.bfloat16)


def solution(mesh):
    in_specs = (
        P("col", "grp"),
        P("grp", None, None),
        P("grp"),
        P("grp"),
        P("grp"),
        P("grp"),
        P(),
        P(),
    )
    out_specs = P(("grp", "col"), None)
    return jax.shard_map(
        per_device, mesh=mesh, in_specs=in_specs, out_specs=out_specs, check_vma=False
    )
```

time: 167 us -> 61.2 us (0.37)
  waiting for transfers between devices: 119 us -> 0.01 us
  blocking collectives: 14.9 us -> 31.6 us
  between operations: 13.4 us -> 0.07 us
  Pallas kernels: 0 us -> 12 us
  matrix products: 8.17 us -> 0.8 us
  local copies, waits for them, and re-layouts: 8.42 us -> 12.6 us
  starting transfers between devices: 0.03 us -> 3.52 us
  other arithmetic: 2.04 us -> 0 us
    all_gather x1 -> x0, waiting for transfers between devices: 119 us -> none  [per_device(): source_table = lax.all_gather(features, 'grp', axis=1, tiled=True)]
    all_to_all x1 -> x2, blocking collectives: 14.9 us -> 31.6 us  [the longest x1 17.8 us: per_device(): rows = lax.all_to_all(aggregated, 'col', 0, 0, tiled=True).reshape(-1, 128)]
    pallas_call x0 -> x3, Pallas kernels: none -> 12 us  [the longest x1 5.91 us: per_device(): pl.pallas_call(local_kernel, name='local', out_shape=(jax.ShapeDtypeStruc...]
    unnamed x8 -> x21, local copies, waits for them, and re-layouts: 0.02 us -> 11.9 us
    gather x2 -> x0, local copies, waits for them, and re-layouts: 8.39 us -> none  [the longest x1 6.59 us: per_device(): picked = jnp.take(source_table, tile_src, axis=1)]
    dot_general x3 -> x1, matrix products: 8.17 us -> 0.8 us  [per_device(): lax.dot_general(rows, weight, (((0,), (0,)), ((), ())), preferred_element...]
    all_to_all x0 -> x1, starting transfers between devices: none -> 3.52 us  [per_device(): lax.all_to_all(blocks, 'grp', 0, 0, tiled=True)]
  transfers between devices with their start and end apart: 1 -> 1, of which waited for: 1 -> 0; matrix products, arithmetic and copies ran while one was open for 2% -> 0% of each run, Pallas kernels for 0% -> 10%
where the time goes in v1:
time: 61.2 us; the launch traced here: 60.6 us
  blocking collectives  31.6 us (52%)
  local copies, waits for them, and re-layouts  12.6 us (21%)
  Pallas kernels  12 us (20%)
  starting transfers between devices  3.52 us (6%)
  matrix products  0.8 us (1%)
    all_to_all x1, blocking collectives, per_device(): rows = lax.all_to_all(aggregated, 'col', 0, 0, tiled=True).reshape(-1, 128)  17.8 us
    all_to_all x1, blocking collectives, per_device(): lax.all_to_all(jnp.broadcast_to(tile_src, (n_grp, n_tiles)), 'grp', 0, 0,...  13.8 us
    unnamed x21, local copies, waits for them, and re-layouts  11.9 us
    pallas_call x1, Pallas kernels, per_device(): pl.pallas_call(local_kernel, name='local', out_shape=(jax.ShapeDtypeStruc...  5.91 us
    pallas_call x1, Pallas kernels, per_device(): pl.pallas_call(remote_kernel, name='remote', out_shape=jax.ShapeDtypeStru...  4.08 us
    all_to_all x1, starting transfers between devices, per_device(): lax.all_to_all(blocks, 'grp', 0, 0, tiled=True)  3.52 us
    pallas_call x1, Pallas kernels, per_device(): pl.pallas_call(gather_kernel, name='gather', out_shape=jax.ShapeDtypeStru...  2.04 us
  transfers between devices with their start and end apart: 1, of which 0 were waited for; matrix products, arithmetic and copies ran while one was open for 0% of the time, Pallas kernels for 10%

profile of v1, /device:TPU:1, one launch (start us, length us, event | category | flops | bytes accessed | tf_op | source)
XLA Modules:
  0.0 60.6 jit_solution(13187010560071713872)
XLA Ops:
  0.0 0.0 copy-start
  0.0 0.7 %broadcast_in_dim.4 = s32[16,1,256]{2,1,0:T(1,128)S(1)} broadcast(s32[256]{0:T(256)} %src_s.1), dimensions={2} | broadcast | bytes 17408 | tf_op jit(solution)/shard_map/broadcast_in_dim | solution.py:151
  0.7 13.8 %all_to_all.18 = s32[16,1,256]{2,1,0:T(1,128)S(1)} all-to-all(s32[16,1,256]{2,1,0:T(1,128)S(1)} %broadcast_in_dim.4), channel_id=1, replica_groups=mesh['grp'=16,'col'=16] {'grp'}, dimensions={0} | all-to-all | bytes 32768 | tf_op jit(solution)/shard_map/all_to_all | solution.py:150
  14.5 0.0 copy-start.3
  14.5 1.2 %copy-done.3 = bf16[8,65536]{1,0:T(8,128)(2,1)S(1)} copy-done((bf16[8,65536]{1,0:T(8,128)(2,1)S(1)}, bf16[8,65536]{1,0:T(8,128)(2,1)}, u32[]{:S(2)}) %copy-start.3) | copy-done | bytes 1048600
  15.8 2.0 %gather.1 = bf16[16,4,8,128]{3,2,1,0:T(8,128)(2,1)} custom-call(s32[16,256]{1,0:T(8,128)S(1)} %bitcast.11, bf16[8,65536]{1,0:T(8,128)(2,1)S(1)} %copy-done.3), custom_call_target="tpu_custom_call" | custom-call | tf_op jit(solution)/shard_map/gather/pallas_call | solution.py:177
  17.8 3.5 %all-to-all-start.1 = ((bf16[16,4,8,128]{3,2,1,0:T(8,128)(2,1)}), bf16[16,4,8,128]{3,2,1,0:T(8,128)(2,1)S(1)}, u32[]{:S(2)}, u32[]{:S(2)}) async-start(bf16[16,4,8,128]{3,2,1,0:T(8,128)(2,1)} %gather.1), calls=%async_computation.1 | async-start | bytes 262144 | tf_op jit(solution)/shard_map/all_to_all | solution.py:190
  21.3 0.0 copy-start.1
  21.4 3.4 %copy-done.1 = bf16[256,128,128]{2,1,0:T(8,128)(2,1)S(1)} copy-done((bf16[256,128,128]{2,1,0:T(8,128)(2,1)S(1)}, bf16[256,128,128]{2,1,0:T(8,128)(2,1)}, u32[]{:S(2)}) %copy-start.1) | copy-done | bytes 8388632
  24.7 0.0 copy-start.4
  24.7 1.2 %copy-done.4 = bf16[8,65536]{1,0:T(8,128)(2,1)S(1)} copy-done((bf16[8,65536]{1,0:T(8,128)(2,1)S(1)}, bf16[8,65536]{1,0:T(8,128)(2,1)}, u32[]{:S(2)}) %copy-start.4) | copy-done | bytes 1048600
  26.0 0.0 copy-start.5
  26.0 0.7 %copy-done.5 = s32[256]{0:T(256)S(1)} copy-done((s32[256]{0:T(256)S(1)}, s32[256]{0:T(256)}, u32[]{:S(2)}) %copy-start.5) | copy-done | bytes 1048
  26.6 0.0 copy-start.6
  26.6 0.7 %copy-done.6 = f32[2048]{0:T(1024)S(1)} copy-done((f32[2048]{0:T(1024)S(1)}, f32[2048]{0:T(1024)}, u32[]{:S(2)}) %copy-start.6) | copy-done | bytes 8216
  27.3 0.0 copy-start.7
  27.3 0.7 %copy-done.7 = s32[256]{0:T(256)S(1)} copy-done((s32[256]{0:T(256)S(1)}, s32[256]{0:T(256)}, u32[]{:S(2)}) %copy-start.7) | copy-done | bytes 1048
  28.0 0.0 copy-start.8
  28.0 0.7 %copy-done.8 = s32[16]{0:T(128)S(1)} copy-done((s32[16]{0:T(128)S(1)}, s32[16]{0:T(128)}, u32[]{:S(2)}) %copy-start.8) | copy-done | bytes 88
  28.7 0.0 copy-start.9
  28.7 5.9 %local.1 = (f32[17,8,128]{2,1,0:T(8,128)S(1)}, s32[272]{0:T(512)S(1)}, s32[1]{0:T(128)}) custom-call(s32[256]{0:T(256)S(1)} %copy-done.5, s32[256]{0:T(256)S(1)} %copy-done.7, s32[16]{0:T(128)S(1)} %copy-done.8, s32[1,256]{1,0:T(1,128)S(1)} %bitcast.12, f32[16,128]{1,0:T(8,128)S(1)} %bitcast.13, bf16[8,65536]{1,0:T(8,128)(2,1)S(1)} %copy-done.4, ...), custom_call_target="tpu_custom_call" | custom-call | flops 268435456 | bytes 9437184 | tf_op jit(solution)/shard_map/local/pallas_call | solution.py:153
  34.6 0.0 all-to-all-done.1
  34.6 0.0 copy-start.2
  34.6 3.4 %copy-done.2 = bf16[256,128,128]{2,1,0:T(8,128)(2,1)S(1)} copy-done((bf16[256,128,128]{2,1,0:T(8,128)(2,1)S(1)}, bf16[256,128,128]{2,1,0:T(8,128)(2,1)}, u32[]{:S(2)}) %copy-start.2) | copy-done | bytes 8388632
  38.0 4.1 %remote.1 = bf16[16,8,128]{2,1,0:T(8,128)(2,1)S(1)} custom-call(s32[272]{0:T(512)S(1)} %get-tuple-element.8.remote_s, s32[1]{0:T(128)} %get-tuple-element.9.counts_s, bf16[64,8,128]{2,1,0:T(8,128)(2,1)S(1)} %bitcast.10, f32[17,8,128]{2,1,0:T(8,128)S(1)} %get-tuple-element.10.acc_in_ref, bf16[256,128,128]{2,1,0:T(8,128)(2,1)S(1)} %copy-done.2), custom_call_target="tpu_custom_call" | custom-call | tf_op jit(solution)/shard_map/remote/pallas_call | solution.py:191
  42.1 17.8 %all_to_all.19 = bf16[16,8,128]{2,1,0:T(8,128)(2,1)S(1)} all-to-all(bf16[16,8,128]{2,1,0:T(8,128)(2,1)S(1)} %remote.1), channel_id=1, replica_groups=mesh['grp'=16,'col'=16] {'col'}, dimensions={0} | all-to-all | bytes 65536 | tf_op jit(solution)/shard_map/all_to_all | solution.py:203
  59.8 0.0 copy-done
  59.8 0.0 copy-done.9
  59.8 0.8 %fusion.1 = bf16[128,128]{1,0:T(8,128)(2,1)} fusion(bf16[128,128]{1,0:T(8,128)(2,1)S(1)} %copy-done, bf16[16,8,128]{2,1,0:T(8,128)(2,1)S(1)} %all_to_all.19, f32[128]{0:T(128)S(1)} %copy-done.9), kind=kOutput, calls=%fused_computation.2 | convolution fusion | flops 4243456 | bytes 98816 | tf_op jit(solution)/shard_map/dot_general | solution.py:205
  (1 shorter events, 0.0 us)
Async XLA Ops:
  0.0 59.8 %copy-start = (bf16[128,128]{1,0:T(8,128)(2,1)S(1)}, bf16[128,128]{1,0:T(8,128)(2,1)}, u32[]{:S(2)}) copy-start(bf16[128,128]{1,0:T(8,128)(2,1)} %param.14) | copy-start | bytes 98308
  14.5 1.2 %copy-start.3 = (bf16[8,65536]{1,0:T(8,128)(2,1)S(1)}, bf16[8,65536]{1,0:T(8,128)(2,1)}, u32[]{:S(2)}) copy-start(bf16[8,65536]{1,0:T(8,128)(2,1)} %feat_ref.3) | copy-start | bytes 3145732
  17.8 16.8 %all-to-all-start.1 = ((bf16[16,4,8,128]{3,2,1,0:T(8,128)(2,1)}), bf16[16,4,8,128]{3,2,1,0:T(8,128)(2,1)S(1)}, u32[]{:S(2)}, u32[]{:S(2)}) async-start(bf16[16,4,8,128]{3,2,1,0:T(8,128)(2,1)} %gather.1), calls=%async_computation.1 | async-start | bytes 262144 | tf_op jit(solution)/shard_map/all_to_all | solution.py:190
  21.3 3.4 %copy-start.1 = (bf16[256,128,128]{2,1,0:T(8,128)(2,1)S(1)}, bf16[256,128,128]{2,1,0:T(8,128)(2,1)}, u32[]{:S(2)}) copy-start(bf16[256,128,128]{2,1,0:T(8,128)(2,1)} %adj_ref.3) | copy-start | bytes 25165828
  24.7 1.2 %copy-start.4 = (bf16[8,65536]{1,0:T(8,128)(2,1)S(1)}, bf16[8,65536]{1,0:T(8,128)(2,1)}, u32[]{:S(2)}) copy-start(bf16[8,65536]{1,0:T(8,128)(2,1)} %feat_ref.3) | copy-start | bytes 3145732
  26.0 0.7 %copy-start.5 = (s32[256]{0:T(256)S(1)}, s32[256]{0:T(256)}, u32[]{:S(2)}) copy-start(s32[256]{0:T(256)} %src_s.1) | copy-start | bytes 3076
  26.6 0.7 %copy-start.6 = (f32[2048]{0:T(1024)S(1)}, f32[2048]{0:T(1024)}, u32[]{:S(2)}) copy-start(f32[2048]{0:T(1024)} %param.13) | copy-start | bytes 24580
  27.3 0.7 %copy-start.7 = (s32[256]{0:T(256)S(1)}, s32[256]{0:T(256)}, u32[]{:S(2)}) copy-start(s32[256]{0:T(256)} %dst_s.1) | copy-start | bytes 3076
  28.0 0.7 %copy-start.8 = (s32[16]{0:T(128)S(1)}, s32[16]{0:T(128)}, u32[]{:S(2)}) copy-start(s32[16]{0:T(128)} %ids_s.1) | copy-start | bytes 196
  28.7 31.2 %copy-start.9 = (f32[128]{0:T(128)S(1)}, f32[128]{0:T(128)}, u32[]{:S(2)}) copy-start(f32[128]{0:T(128)} %param.15) | copy-start | bytes 1540
  34.6 3.4 %copy-start.2 = (bf16[256,128,128]{2,1,0:T(8,128)(2,1)S(1)}, bf16[256,128,128]{2,1,0:T(8,128)(2,1)}, u32[]{:S(2)}) copy-start(bf16[256,128,128]{2,1,0:T(8,128)(2,1)} %adj_ref.3) | copy-start | bytes 25165828

commit v2 on v1

v2 whole, which is shorter than its diff:
```python
import jax
import jax.numpy as jnp
from jax import lax
from jax.experimental import pallas as pl
from jax.experimental.pallas import tpu as pltpu
from jax.sharding import PartitionSpec as P

NEED = 4
BATCH = 32
HELD = 64
CHUNK = 32
BIG = 1 << 30

VMEM = pl.BlockSpec(memory_space=pltpu.VMEM)
SMEM = pl.BlockSpec(memory_space=pltpu.SMEM)
HBM = pl.BlockSpec(memory_space=pltpu.HBM)


def four_least(values):
    least = []
    for _ in range(NEED):
        low = jnp.min(values, axis=1, keepdims=True)
        least.append(low)
        values = jnp.where(values > low, values, BIG)
    return least


def tile_products(entries, first, last, load_x, load_tile, acc_ref, before=None):
    zero = jnp.zeros((8, 128), jnp.float32)

    def one_pass(step, carry):
        if before is not None:
            carry = before(entries[step * BATCH + BATCH - 1] & 255, carry)
        results = []
        for pair in range(BATCH // 2):
            tiles, xs, dsts = [], [], []
            for q in range(2):
                entry = entries[step * BATCH + pair * 2 + q]
                tiles.append(load_tile(entry & 255))
                xs.append(load_x(entry >> 13))
                dsts.append((entry >> 8) & 31)
            left = jnp.concatenate([xs[0], zero], axis=0)
            right = jnp.concatenate([zero, xs[1]], axis=0)
            lhs = jnp.concatenate([left, right], axis=1).astype(jnp.bfloat16)
            rhs = jnp.concatenate(tiles, axis=1)
            out = lax.dot_general(
                lhs, rhs, (((1,), (1,)), ((), ())), preferred_element_type=jnp.float32
            )
            results += [(dsts[0], out[0:8]), (dsts[1], out[8:16])]
        for dst, value in results:
            acc_ref[dst] += value
        return carry

    return lax.fori_loop(first // BATCH, (last + BATCH - 1) // BATCH, one_pass, 0)


def local_kernel(
    src_h, src_row_h, dst_h, ids_h, coef_h, feat_h, adj_h,
    acc_ref, feat_ref, held_ref, remote_s,
    adj_ref, src_s, src_v, dst_s, ids_s, coef_ref, local_s, slot_v, slot_s, sems,
):
    copies = [
        pltpu.make_async_copy(a, b, sems.at[i])
        for i, (a, b) in enumerate(
            [
                (src_row_h, src_v), (src_h, src_s), (dst_h, dst_s), (ids_h, ids_s),
                (coef_h, coef_ref), (feat_h, feat_ref), (adj_h, adj_ref),
                (adj_h.at[pl.ds(0, HELD)], held_ref), (slot_v, slot_s),
            ]
        )
    ]
    for copy in copies[:-1]:
        copy.start()
    n_tiles = src_s.shape[0]
    group = lax.axis_index("grp")
    group_len = feat_ref.shape[1] // 128
    n_dst = ids_s.shape[0]
    n_grp = lax.axis_size("grp")
    shift = group_len.bit_length() - 1
    copies[0].wait()
    src = jnp.broadcast_to(src_v[...], (n_grp, n_tiles))
    mine = (src >> shift) == lax.broadcasted_iota(jnp.int32, (n_grp, n_tiles), 0)
    least = four_least(jnp.where(mine, src, BIG))
    rank = jnp.zeros((n_grp, n_tiles), jnp.int32)
    for low in least[: NEED - 1]:
        rank += jnp.where(mine & (src > low), 1, 0)
    slot_v[...] = (src_v[...] >> shift) * NEED + jnp.sum(rank, axis=0, keepdims=True)
    copies[-1].start()
    for copy in copies[1:5] + copies[-1:]:
        copy.wait()

    def sort_out(t, carry):
        n_local, n_remote = carry
        source = src_s[t]
        head = t + dst_s[t] * 256
        is_local = jnp.where((source >> shift) == group, 1, 0)
        local_s[n_local] = head + (source & (group_len - 1)) * 8192
        remote_s[n_remote] = head + slot_s[0, t] * 8192
        return n_local + is_local, n_remote + 1 - is_local

    n_local, n_early = lax.fori_loop(0, HELD, sort_out, (0, 0), unroll=8)
    for i in range(BATCH):
        remote_s[n_early + i] = n_dst * 256
    late = (n_early + BATCH - 1) // BATCH * BATCH
    n_local, n_late = lax.fori_loop(HELD, n_tiles, sort_out, (n_local, late), unroll=8)
    for i in range(BATCH):
        local_s[n_local + i] = n_dst * 256
        remote_s[n_late + i] = n_dst * 256 + n_tiles - 1
    remote_s[remote_s.shape[0] - 2] = late
    remote_s[remote_s.shape[0] - 1] = n_late
    copies[5].wait()
    for d in range(n_dst):
        place = pl.multiple_of((ids_s[d] - group * group_len) * 128, 128)
        own = feat_ref[:, pl.ds(place, 128)].astype(jnp.float32)
        acc_ref[d] = coef_ref[d : d + 1, :] * own
    acc_ref[n_dst] = jnp.zeros((8, 128), jnp.float32)
    copies[6].wait()

    def load_x(place):
        return feat_ref[:, pl.ds(pl.multiple_of(place * 128, 128), 128)].astype(jnp.float32)

    tile_products(local_s, 0, n_local, load_x, adj_ref.__getitem__, acc_ref)
    copies[7].wait()


def gather_kernel(req_ref, feat_ref, out_ref, place_v, place_s, sem):
    group = lax.axis_index("grp")
    group_len = feat_ref.shape[1] // 128
    shift = group_len.bit_length() - 1
    n_grp, n_tiles = req_ref.shape
    req = req_ref[...]
    least = four_least(jnp.where((req >> shift) == group, req & (group_len - 1), BIG))
    lane = lax.broadcasted_iota(jnp.int32, (n_grp, 128), 1)
    table = jnp.zeros((n_grp, 128), jnp.int32)
    for r, low in enumerate(least):
        table = jnp.where(lane == r, jnp.minimum(low, group_len - 1), table)
    place_v[...] = table
    copy = pltpu.make_async_copy(place_v, place_s, sem)
    copy.start()
    copy.wait()
    for k in range(n_grp):
        for r in range(NEED):
            place = pl.multiple_of(place_s[k, r] * 128, 128)
            out_ref[k, r] = feat_ref[:, pl.ds(place, 128)]


def remote_kernel(
    remote_s, recv_ref, acc_in_ref, held_ref, adj_h, out_ref, adj_ref, acc_ref, x_ref, sems
):
    n_tiles = adj_h.shape[0]
    n_chunks = (n_tiles - HELD) // CHUNK

    def chunk(i):
        first = pl.multiple_of(i * CHUNK, CHUNK)
        return pltpu.make_async_copy(
            adj_h.at[pl.ds(first + HELD, CHUNK)], adj_ref.at[pl.ds(first, CHUNK)], sems.at[i]
        )

    def start(i, carry):
        chunk(i).start()
        return carry

    def wait(i, carry):
        chunk(i).wait()
        return carry

    def arrived(tile, ready):
        needed = jnp.maximum(ready, (tile - HELD) // CHUNK + 1)
        lax.fori_loop(ready, needed, wait, 0)
        return needed

    lax.fori_loop(0, n_chunks, start, 0, unroll=True)
    acc_ref[...] = acc_in_ref[...]
    x_ref[...] = recv_ref[...].astype(jnp.float32)
    late = remote_s[remote_s.shape[0] - 2]
    tile_products(remote_s, 0, late, x_ref.__getitem__, held_ref.__getitem__, acc_ref)
    ready = tile_products(
        remote_s, late, remote_s[remote_s.shape[0] - 1], x_ref.__getitem__,
        lambda tile: adj_ref[tile - HELD], acc_ref, arrived,
    )
    lax.fori_loop(ready, n_chunks, wait, 0)
    out_ref[...] = acc_ref[: out_ref.shape[0]].astype(out_ref.dtype)


def per_device(features, adj_tiles, tile_dst, tile_src, dst_ids, self_coef, weight, out_bias):
    n_feat = features.shape[0]
    n_tiles = tile_src.shape[0]
    n_dst = dst_ids.shape[0]
    n_grp = lax.axis_size("grp")
    n_slots = n_grp * NEED
    params = pltpu.CompilerParams(vmem_limit_bytes=16 << 20)
    requests = lax.all_to_all(
        jnp.broadcast_to(tile_src, (n_grp, n_tiles)), "grp", 0, 0, tiled=True
    )
    acc, feat_held, adj_held, remote = pl.pallas_call(
        local_kernel,
        name="local",
        out_shape=(
            pltpu.VMEM((n_dst + 1, n_feat, 128), jnp.float32),
            pltpu.VMEM(features.shape, features.dtype),
            pltpu.VMEM((HELD,) + adj_tiles.shape[1:], adj_tiles.dtype),
            pltpu.SMEM((n_tiles + 2 * BATCH + 2,), jnp.int32),
        ),
        in_specs=[HBM] * 7,
        out_specs=(VMEM, VMEM, VMEM, SMEM),
        scratch_shapes=[
            pltpu.VMEM(adj_tiles.shape, adj_tiles.dtype),
            pltpu.SMEM((n_tiles,), jnp.int32),
            pltpu.VMEM((1, n_tiles), jnp.int32),
            pltpu.SMEM((n_tiles,), jnp.int32),
            pltpu.SMEM((n_dst,), jnp.int32),
            pltpu.VMEM((n_dst, 128), jnp.float32),
            pltpu.SMEM((n_tiles + BATCH,), jnp.int32),
            pltpu.VMEM((1, n_tiles), jnp.int32),
            pltpu.SMEM((1, n_tiles), jnp.int32),
            pltpu.SemaphoreType.DMA((9,)),
        ],
        compiler_params=params,
        cost_estimate=pl.CostEstimate(
            flops=2 * n_tiles * 128 * 128 * 32, bytes_accessed=18 << 20, transcendentals=0
        ),
    )(
        *[
            pltpu.with_memory_space_constraint(a, pltpu.HBM)
            for a in (
                tile_src, tile_src.reshape(1, n_tiles), tile_dst, dst_ids,
                self_coef.reshape(n_dst, 128), features, adj_tiles,
            )
        ]
    )
    blocks = pl.pallas_call(
        gather_kernel,
        name="gather",
        out_shape=jax.ShapeDtypeStruct((n_grp, NEED, n_feat, 128), features.dtype),
        in_specs=[VMEM, VMEM],
        out_specs=VMEM,
        scratch_shapes=[
            pltpu.VMEM((n_grp, 128), jnp.int32),
            pltpu.SMEM((n_grp, 128), jnp.int32),
            pltpu.SemaphoreType.DMA,
        ],
        compiler_params=params,
    )(requests, pltpu.with_memory_space_constraint(feat_held, pltpu.VMEM))
    arrived = lax.all_to_all(blocks, "grp", 0, 0, tiled=True).reshape(n_slots, n_feat, 128)
    aggregated = pl.pallas_call(
        remote_kernel,
        name="remote",
        out_shape=jax.ShapeDtypeStruct((n_dst, n_feat, 128), jnp.bfloat16),
        in_specs=[SMEM, VMEM, VMEM, VMEM, HBM],
        out_specs=VMEM,
        scratch_shapes=[
            pltpu.VMEM((n_tiles - HELD,) + adj_tiles.shape[1:], adj_tiles.dtype),
            pltpu.VMEM((n_dst + 1, n_feat, 128), jnp.float32),
            pltpu.VMEM((n_slots, n_feat, 128), jnp.float32),
            pltpu.SemaphoreType.DMA(((n_tiles - HELD) // CHUNK,)),
        ],
        compiler_params=params,
    )(
        remote, arrived, pltpu.with_memory_space_constraint(acc, pltpu.VMEM),
        pltpu.with_memory_space_constraint(adj_held, pltpu.VMEM),
        pltpu.with_memory_space_constraint(adj_tiles, pltpu.HBM),
    )
    rows = lax.all_to_all(aggregated, "col", 0, 0, tiled=True).reshape(-1, 128)
    mixed = (
        lax.dot_general(
            rows, weight, (((0,), (0,)), ((), ())), preferred_element_type=jnp.float32
        )
        + out_bias
    )
    return jax.nn.relu(mixed).astype(jnp.bfloat16)


def solution(mesh):
    in_specs = (
        P("col", "grp"),
        P("grp", None, None),
        P("grp"),
        P("grp"),
        P("grp"),
        P("grp"),
        P(),
        P(),
    )
    out_specs = P(("grp", "col"), None)
    return jax.shard_map(
        per_device, mesh=mesh, in_specs=in_specs, out_specs=out_specs, check_vma=False
    )
```

time: 61.2 us -> 51.6 us (0.84)
  local copies, waits for them, and re-layouts: 12.6 us -> 1.31 us
  starting transfers between devices: 3.52 us -> 7.58 us
  Pallas kernels: 12 us -> 9.89 us
  blocking collectives: 31.6 us -> 30.2 us
  waiting for transfers between devices: 0.01 us -> 1.39 us
    unnamed x21 -> x5, local copies, waits for them, and re-layouts: 11.9 us -> 0.01 us
    all_to_all x1, starting transfers between devices: 3.52 us -> 7.58 us  [per_device(): lax.all_to_all(jnp.broadcast_to(tile_src, (n_grp, n_tiles)), 'grp', 0, 0,...]
    all_to_all x1, blocking collectives: 13.8 us -> 11.9 us  [per_device(): lax.all_to_all(blocks, 'grp', 0, 0, tiled=True)]
    all_to_all x1, waiting for transfers between devices: 0.01 us -> 1.39 us  [per_device(): lax.all_to_all(jnp.broadcast_to(tile_src, (n_grp, n_tiles)), 'grp', 0, 0,...]
    pallas_call x1, Pallas kernels: 5.91 us -> 5.04 us  [per_device(): pl.pallas_call(local_kernel, name='local', out_shape=(pltpu.VMEM((n_dst +...]
    pallas_call x1, Pallas kernels: 2.04 us -> 1.4 us  [per_device(): pl.pallas_call(gather_kernel, name='gather', out_shape=jax.ShapeDtypeStru...]
    pallas_call x1, Pallas kernels: 4.08 us -> 3.45 us  [per_device(): pl.pallas_call(remote_kernel, name='remote', out_shape=jax.ShapeDtypeStru...]
  transfers between devices with their start and end apart: 1 -> 1, of which waited for: 0 -> 1; matrix products, arithmetic and copies ran while one was open for 0% -> 0% of each run, Pallas kernels for 10% -> 10%
where the time goes in v2:
time: 51.6 us; the launch traced here: 51.2 us
  blocking collectives  30.2 us (59%)
  Pallas kernels  9.89 us (19%)
  starting transfers between devices  7.58 us (15%)
  waiting for transfers between devices  1.39 us (3%)
  local copies, waits for them, and re-layouts  1.31 us (3%)
  matrix products  0.8 us (2%)
    all_to_all x1, blocking collectives, per_device(): rows = lax.all_to_all(aggregated, 'col', 0, 0, tiled=True).reshape(-1, 128)  18.3 us
    all_to_all x1, blocking collectives, per_device(): lax.all_to_all(blocks, 'grp', 0, 0, tiled=True)  11.9 us
    all_to_all x1, starting transfers between devices, per_device(): lax.all_to_all(jnp.broadcast_to(tile_src, (n_grp, n_tiles)), 'grp', 0, 0,...  7.58 us
    pallas_call x1, Pallas kernels, per_device(): pl.pallas_call(local_kernel, name='local', out_shape=(pltpu.VMEM((n_dst +...  5.04 us
    pallas_call x1, Pallas kernels, per_device(): pl.pallas_call(remote_kernel, name='remote', out_shape=jax.ShapeDtypeStru...  3.45 us
    pallas_call x1, Pallas kernels, per_device(): pl.pallas_call(gather_kernel, name='gather', out_shape=jax.ShapeDtypeStru...  1.4 us
    all_to_all x1, waiting for transfers between devices, per_device(): lax.all_to_all(jnp.broadcast_to(tile_src, (n_grp, n_tiles)), 'grp', 0, 0,...  1.39 us
    broadcast_in_dim x1, local copies, waits for them, and re-layouts, per_device(): jnp.broadcast_to(tile_src, (n_grp, n_tiles))  1.3 us
  transfers between devices with their start and end apart: 1, of which 1 were waited for; matrix products, arithmetic and copies ran while one was open for 0% of the time, Pallas kernels for 10%

profile of v2, /device:TPU:1, one launch (start us, length us, event | category | flops | bytes accessed | tf_op | source)
XLA Modules:
  0.0 51.2 jit_solution(1692607136333608478)
XLA Ops:
  0.0 0.0 copy-start
  0.0 1.3 %broadcast_in_dim.4 = s32[16,1,256]{2,1,0:T(1,128)} broadcast(s32[256]{0:T(256)} %src_h.1), dimensions={2} | broadcast | bytes 17408 | tf_op jit(solution)/shard_map/broadcast_in_dim | solution.py:193
  1.3 7.6 %all-to-all-start = ((s32[16,1,256]{2,1,0:T(1,128)}), s32[16,1,256]{2,1,0:T(1,128)S(1)}, u32[]{:S(2)}, u32[]{:S(2)}) async-start(s32[16,1,256]{2,1,0:T(1,128)} %broadcast_in_dim.4), calls=%async_computation | async-start | bytes 32768 | tf_op jit(solution)/shard_map/all_to_all | solution.py:192
  8.9 5.0 %local.1 = (f32[17,8,128]{2,1,0:T(8,128)S(1)}, bf16[8,65536]{1,0:T(8,128)(2,1)S(1)}, bf16[64,128,128]{2,1,0:T(8,128)(2,1)S(1)}, s32[322]{0:T(512)S(4)}) custom-call(s32[256]{0:T(256)} %src_h.1, s32[1,256]{1,0:T(1,128)} %bitcast.12, s32[256]{0:T(256)} %dst_h.1, s32[16]{0:T(128)} %ids_h.1, f32[16,128]{1,0:T(8,128)} %bitcast.13, bf16[8,65536]{1,0:T(8,128)(2,1)} %feat_h.1, ...), custom_call_target="tpu_custom_call" | custom-call | flops 268435456 | bytes 18874368 | tf_op jit(solution)/shard_map/local/pallas_call | solution.py:195
  13.9 0.0 copy-start.1
  14.0 1.4 %all-to-all-done = s32[16,1,256]{2,1,0:T(1,128)S(1)} async-done(((s32[16,1,256]{2,1,0:T(1,128)}), s32[16,1,256]{2,1,0:T(1,128)S(1)}, u32[]{:S(2)}, u32[]{:S(2)}) %all-to-all-start) | async-done | bytes 16416 | tf_op jit(solution)/shard_map/all_to_all | solution.py:192
  15.3 1.4 %gather.1 = bf16[16,4,8,128]{3,2,1,0:T(8,128)(2,1)S(1)} custom-call(s32[16,256]{1,0:T(8,128)S(1)} %bitcast.11, bf16[8,65536]{1,0:T(8,128)(2,1)S(1)} %get-tuple-element.10.feat_ref), custom_call_target="tpu_custom_call" | custom-call | tf_op jit(solution)/shard_map/gather/pallas_call | solution.py:231
  16.8 11.9 %all_to_all.18 = bf16[16,4,8,128]{3,2,1,0:T(8,128)(2,1)S(1)} all-to-all(bf16[16,4,8,128]{3,2,1,0:T(8,128)(2,1)S(1)} %gather.1), channel_id=1, replica_groups=mesh['grp'=16,'col'=16] {'grp'}, dimensions={0} | all-to-all | bytes 262144 | tf_op jit(solution)/shard_map/all_to_all | solution.py:244
  28.7 3.4 %remote.1 = bf16[16,8,128]{2,1,0:T(8,128)(2,1)S(1)} custom-call(s32[322]{0:T(512)S(4)} %get-tuple-element.9.remote_s, bf16[64,8,128]{2,1,0:T(8,128)(2,1)S(1)} %bitcast.10, f32[17,8,128]{2,1,0:T(8,128)S(1)} %get-tuple-element.11.acc_in_ref, bf16[64,128,128]{2,1,0:T(8,128)(2,1)S(1)} %get-tuple-element.12.held_ref, bf16[256,128,128]{2,1,0:T(8,128)(2,1)} %adj_h.3), custom_call_target="tpu_custom_call" | custom-call | tf_op jit(solution)/shard_map/remote/pallas_call | solution.py:245
  32.1 18.3 %all_to_all.19 = bf16[16,8,128]{2,1,0:T(8,128)(2,1)S(1)} all-to-all(bf16[16,8,128]{2,1,0:T(8,128)(2,1)S(1)} %remote.1), channel_id=1, replica_groups=mesh['grp'=16,'col'=16] {'col'}, dimensions={0} | all-to-all | bytes 65536 | tf_op jit(solution)/shard_map/all_to_all | solution.py:263
  50.4 0.0 copy-done
  50.4 0.0 copy-done.1
  50.4 0.8 %fusion.1 = bf16[128,128]{1,0:T(8,128)(2,1)} fusion(bf16[128,128]{1,0:T(8,128)(2,1)S(1)} %copy-done, bf16[16,8,128]{2,1,0:T(8,128)(2,1)S(1)} %all_to_all.19, f32[128]{0:T(128)S(1)} %copy-done.1), kind=kOutput, calls=%fused_computation.2 | convolution fusion | flops 4243456 | bytes 98816 | tf_op jit(solution)/shard_map/dot_general | solution.py:265
  (1 shorter events, 0.0 us)
Async XLA Ops:
  0.0 50.4 %copy-start = (bf16[128,128]{1,0:T(8,128)(2,1)S(1)}, bf16[128,128]{1,0:T(8,128)(2,1)}, u32[]{:S(2)}) copy-start(bf16[128,128]{1,0:T(8,128)(2,1)} %param.14) | copy-start | bytes 98308
  1.3 14.0 %all-to-all-start = ((s32[16,1,256]{2,1,0:T(1,128)}), s32[16,1,256]{2,1,0:T(1,128)S(1)}, u32[]{:S(2)}, u32[]{:S(2)}) async-start(s32[16,1,256]{2,1,0:T(1,128)} %broadcast_in_dim.4), calls=%async_computation | async-start | bytes 32768 | tf_op jit(solution)/shard_map/all_to_all | solution.py:192
  13.9 36.5 %copy-start.1 = (f32[128]{0:T(128)S(1)}, f32[128]{0:T(128)}, u32[]{:S(2)}) copy-start(f32[128]{0:T(128)} %param.15) | copy-start | bytes 1540

commit v3 on v2

v3 whole, which is shorter than its diff:
```python
import jax
import jax.numpy as jnp
from jax import lax
from jax.experimental import pallas as pl
from jax.experimental.pallas import tpu as pltpu
from jax.sharding import PartitionSpec as P

NEED = 4
BATCH = 32
HELD = 96
FETCH = 8
PAD = 40
CHUNK = 16
EARLY = 2
BIG = 1 << 30
LOCAL_BIT = 24
LOCAL = 1 << LOCAL_BIT

VMEM = pl.BlockSpec(memory_space=pltpu.VMEM)
SMEM = pl.BlockSpec(memory_space=pltpu.SMEM)
HBM = pl.BlockSpec(memory_space=pltpu.HBM)


def four_least(values):
    least = []
    for _ in range(NEED):
        low = jnp.min(values, axis=1, keepdims=True)
        least.append(low)
        values = jnp.where(values > low, values, BIG)
    return least


def tile_pass(entries, first, count, load_x, load_tile, acc_ref):
    zero = jnp.zeros((8, 128), jnp.float32)
    results = []
    for pair in range(count // 2):
        tiles, xs, dsts = [], [], []
        for q in range(2):
            index = first + pair * 2 + q
            entry = entries[index]
            tiles.append(load_tile(index, entry & 255))
            xs.append(load_x((entry >> 13) & 2047))
            dsts.append((entry >> 8) & 31)
        left = jnp.concatenate([xs[0], zero], axis=0)
        right = jnp.concatenate([zero, xs[1]], axis=0)
        lhs = jnp.concatenate([left, right], axis=1).astype(jnp.bfloat16)
        rhs = jnp.concatenate(tiles, axis=1)
        out = lax.dot_general(
            lhs, rhs, (((1,), (1,)), ((), ())), preferred_element_type=jnp.float32
        )
        results += [(dsts[0], out[0:8]), (dsts[1], out[8:16])]
    for dst, value in results:
        acc_ref[dst] += value


def tile_passes(entries, first, last, load_x, load_tile, acc_ref, wait_until, ready):
    def one_pass(step, ready):
        ready = wait_until(entries[step * BATCH + BATCH - 1] & 255, ready)
        tile_pass(entries, step * BATCH, BATCH, load_x, load_tile, acc_ref)
        return ready

    return lax.fori_loop(first, last, one_pass, ready)


def chunked_fetch(adj_h, adj_ref, sems):
    def chunk(i):
        tiles = pl.ds(pl.multiple_of(i * CHUNK, CHUNK), CHUNK)
        return pltpu.make_async_copy(adj_h.at[tiles], adj_ref.at[tiles], sems.at[i])

    def start(i, carry):
        chunk(i).start()
        return carry

    def wait(i, carry):
        chunk(i).wait()
        return carry

    def wait_until(tile, ready):
        needed = jnp.maximum(ready, tile // CHUNK + 1)
        lax.fori_loop(ready, needed, wait, 0)
        return needed

    return start, wait, wait_until


def local_kernel(
    src_h, dst_h, ids_h, coef_h, feat_h, adj_h,
    acc_ref, held_ref, remote_s,
    feat_ref, adj_ref, src_v, dst_v, ids_s, coef_ref, local_s, entry_v, entry_s, sems, adj_sems,
):
    copies = [
        pltpu.make_async_copy(a, b, sems.at[i])
        for i, (a, b) in enumerate(
            [
                (src_h, src_v), (dst_h, dst_v), (ids_h, ids_s), (coef_h, coef_ref),
                (feat_h, feat_ref), (entry_v, entry_s),
            ]
        )
    ]
    for copy in copies[:-1]:
        copy.start()
    n_tiles = src_v.shape[1]
    n_chunks = n_tiles // CHUNK
    fetch, wait, wait_until = chunked_fetch(adj_h, adj_ref, adj_sems)
    for i in range(EARLY):
        fetch(i, 0)
    group = lax.axis_index("grp")
    group_len = feat_ref.shape[1] // 128
    n_dst = ids_s.shape[0]
    n_grp = lax.axis_size("grp")
    shift = group_len.bit_length() - 1
    copies[0].wait()
    copies[1].wait()
    row = src_v[...]
    src = jnp.broadcast_to(row, (n_grp, n_tiles))
    mine = (src >> shift) == lax.broadcasted_iota(jnp.int32, (n_grp, n_tiles), 0)
    least = four_least(jnp.where(mine, src, BIG))
    rank = jnp.zeros((n_grp, n_tiles), jnp.int32)
    for low in least[: NEED - 1]:
        rank += jnp.where(mine & (src > low), 1, 0)
    slot = (row >> shift) * NEED + jnp.sum(rank, axis=0, keepdims=True)
    head = lax.broadcasted_iota(jnp.int32, (1, n_tiles), 1) + dst_v[...] * 256
    entry_v[...] = head + jnp.where(
        (row >> shift) == group, (row & (group_len - 1)) * 8192 + LOCAL, slot * 8192
    )
    copies[-1].start()
    for i in range(EARLY, n_chunks):
        fetch(i, 0)
    copies[-1].wait()

    def sort_out(t, n_local):
        entry = entry_s[0, t]
        local_s[n_local] = entry
        remote_s[t - n_local] = entry
        return n_local + (entry >> LOCAL_BIT)

    n_local = lax.fori_loop(0, n_tiles, sort_out, 0, unroll=16)
    n_remote = n_tiles - n_local
    for i in range(PAD):
        local_s[n_local + i] = n_dst * 256 + n_tiles - 1
        remote_s[n_remote + i] = n_dst * 256 + n_tiles - 1
    remote_s[remote_s.shape[0] - 1] = n_remote
    copies[2].wait()
    copies[3].wait()
    copies[4].wait()
    for d in range(n_dst):
        place = pl.multiple_of((ids_s[d] - group * group_len) * 128, 128)
        own = feat_ref[:, pl.ds(place, 128)].astype(jnp.float32)
        acc_ref[d] = coef_ref[d : d + 1, :] * own
    acc_ref[n_dst] = jnp.zeros((8, 128), jnp.float32)
    def load_x(place):
        return feat_ref[:, pl.ds(pl.multiple_of(place * 128, 128), 128)].astype(jnp.float32)

    ready = tile_passes(
        local_s, 0, (n_local + BATCH - 1) // BATCH, load_x, lambda _, tile: adj_ref[tile],
        acc_ref, wait_until, 0,
    )
    lax.fori_loop(ready, n_chunks, wait, 0)

    def hold(i, carry):
        held_ref[i] = adj_ref[remote_s[i] & 255]
        return carry

    lax.fori_loop(0, HELD, hold, 0, unroll=8)


def gather_kernel(req_ref, feat_h, out_ref, feat_ref, place_v, place_s, sems):
    fetch = pltpu.make_async_copy(feat_h, feat_ref, sems.at[0])
    fetch.start()
    group = lax.axis_index("grp")
    group_len = feat_ref.shape[1] // 128
    shift = group_len.bit_length() - 1
    n_grp, n_tiles = req_ref.shape
    req = req_ref[...]
    least = four_least(jnp.where((req >> shift) == group, req & (group_len - 1), BIG))
    lane = lax.broadcasted_iota(jnp.int32, (n_grp, 128), 1)
    table = jnp.zeros((n_grp, 128), jnp.int32)
    for r, low in enumerate(least):
        table = jnp.where(lane == r, jnp.minimum(low, group_len - 1), table)
    place_v[...] = table
    copy = pltpu.make_async_copy(place_v, place_s, sems.at[1])
    copy.start()
    copy.wait()
    fetch.wait()
    for k in range(n_grp):
        for r in range(NEED):
            place = pl.multiple_of(place_s[k, r] * 128, 128)
            out_ref[k, r] = feat_ref[:, pl.ds(place, 128)]


def remote_kernel(
    remote_s, recv_ref, acc_in_ref, held_ref, adj_h, out_ref, adj_ref, acc_ref, sems
):
    n_remote = remote_s[remote_s.shape[0] - 1]

    def fetch(i, sem):
        pltpu.make_async_copy(adj_h.at[remote_s[i] & 255], adj_ref.at[i - HELD], sem).start()

    def arrive(first, count, sem):
        tiles = pl.ds(first - HELD, count)
        pltpu.make_async_copy(adj_h.at[pl.ds(0, count)], adj_ref.at[tiles], sem).wait()

    def fetch_pass(step, carry):
        def some(i, c):
            for q in range(FETCH):
                fetch(step * BATCH + i * FETCH + q, sems.at[step])
            return c

        return lax.fori_loop(0, BATCH // FETCH, some, carry)

    n_passes = (n_remote + BATCH - 1) // BATCH
    lax.fori_loop(HELD // BATCH, n_passes, fetch_pass, 0)
    acc_ref[...] = acc_in_ref[...]

    def load_x(slot):
        return recv_ref[slot].astype(jnp.float32)

    def late_pass(step, carry):
        arrive(pl.multiple_of(step * BATCH, BATCH), BATCH, sems.at[step])
        tile_pass(
            remote_s, step * BATCH, BATCH, load_x, lambda index, _: adj_ref[index - HELD], acc_ref
        )
        return carry

    tile_pass(remote_s, 0, HELD, load_x, lambda index, _: held_ref[index], acc_ref)
    lax.fori_loop(HELD // BATCH, n_passes, late_pass, 0)
    out_ref[...] = acc_ref[: out_ref.shape[0]].astype(out_ref.dtype)


def per_device(features, adj_tiles, tile_dst, tile_src, dst_ids, self_coef, weight, out_bias):
    n_feat = features.shape[0]
    n_tiles = tile_src.shape[0]
    n_dst = dst_ids.shape[0]
    n_grp = lax.axis_size("grp")
    n_slots = n_grp * NEED
    params = pltpu.CompilerParams(vmem_limit_bytes=16 << 20)
    requests = lax.all_to_all(
        jnp.broadcast_to(tile_src, (n_grp, n_tiles)), "grp", 0, 0, tiled=True
    )
    acc, adj_held, remote = pl.pallas_call(
        local_kernel,
        name="local",
        out_shape=(
            pltpu.VMEM((n_dst + 1, n_feat, 128), jnp.float32),
            pltpu.VMEM((HELD,) + adj_tiles.shape[1:], adj_tiles.dtype),
            pltpu.SMEM((n_tiles + PAD + 1,), jnp.int32),
        ),
        in_specs=[HBM] * 6,
        out_specs=(VMEM, VMEM, SMEM),
        scratch_shapes=[
            pltpu.VMEM(features.shape, features.dtype),
            pltpu.VMEM(adj_tiles.shape, adj_tiles.dtype),
            pltpu.VMEM((1, n_tiles), jnp.int32),
            pltpu.VMEM((1, n_tiles), jnp.int32),
            pltpu.SMEM((n_dst,), jnp.int32),
            pltpu.VMEM((n_dst, 128), jnp.float32),
            pltpu.SMEM((n_tiles + PAD,), jnp.int32),
            pltpu.VMEM((1, n_tiles), jnp.int32),
            pltpu.SMEM((1, n_tiles), jnp.int32),
            pltpu.SemaphoreType.DMA((6,)),
            pltpu.SemaphoreType.DMA((n_tiles // CHUNK,)),
        ],
        compiler_params=params,
        cost_estimate=pl.CostEstimate(
            flops=2 * n_tiles * 128 * 128 * 32, bytes_accessed=18 << 20, transcendentals=0
        ),
    )(
        *[
            pltpu.with_memory_space_constraint(a, pltpu.HBM)
            for a in (
                tile_src.reshape(1, n_tiles), tile_dst.reshape(1, n_tiles), dst_ids,
                self_coef.reshape(n_dst, 128), features, adj_tiles,
            )
        ]
    )
    blocks = pl.pallas_call(
        gather_kernel,
        name="gather",
        out_shape=jax.ShapeDtypeStruct((n_grp, NEED, n_feat, 128), features.dtype),
        in_specs=[VMEM, HBM],
        out_specs=VMEM,
        scratch_shapes=[
            pltpu.VMEM(features.shape, features.dtype),
            pltpu.VMEM((n_grp, 128), jnp.int32),
            pltpu.SMEM((n_grp, 128), jnp.int32),
            pltpu.SemaphoreType.DMA((2,)),
        ],
        compiler_params=params,
    )(requests, pltpu.with_memory_space_constraint(features, pltpu.HBM))
    arrived = lax.all_to_all(blocks, "grp", 0, 0, tiled=True).reshape(n_slots, n_feat, 128)
    aggregated = pl.pallas_call(
        remote_kernel,
        name="remote",
        out_shape=jax.ShapeDtypeStruct((n_dst, n_feat, 128), jnp.bfloat16),
        in_specs=[SMEM, VMEM, VMEM, VMEM, HBM],
        out_specs=VMEM,
        scratch_shapes=[
            pltpu.VMEM((n_tiles - HELD,) + adj_tiles.shape[1:], adj_tiles.dtype),
            pltpu.VMEM((n_dst + 1, n_feat, 128), jnp.float32),
            pltpu.SemaphoreType.DMA((n_tiles // BATCH,)),
        ],
        compiler_params=params,
    )(
        remote, arrived, pltpu.with_memory_space_constraint(acc, pltpu.VMEM),
        pltpu.with_memory_space_constraint(adj_held, pltpu.VMEM),
        pltpu.with_memory_space_constraint(adj_tiles, pltpu.HBM),
    )
    rows = lax.all_to_all(aggregated, "col", 0, 0, tiled=True).reshape(-1, 128)
    mixed = (
        lax.dot_general(
            rows, weight, (((0,), (0,)), ((), ())), preferred_element_type=jnp.float32
        )
        + out_bias
    )
    return jax.nn.relu(mixed).astype(jnp.bfloat16)


def solution(mesh):
    in_specs = (
        P("col", "grp"),
        P("grp", None, None),
        P("grp"),
        P("grp"),
        P("grp"),
        P("grp"),
        P(),
        P(),
    )
    out_specs = P(("grp", "col"), None)
    return jax.shard_map(
        per_device, mesh=mesh, in_specs=in_specs, out_specs=out_specs, check_vma=False
    )
```

time: 51.6 us -> 49.5 us (0.959)
  starting transfers between devices: 7.58 us -> 3.52 us
  blocking collectives: 30.2 us -> 32.7 us
  Pallas kernels: 9.89 us -> 9.26 us
  local copies, waits for them, and re-layouts: 1.31 us -> 0.71 us
    all_to_all x1, starting transfers between devices: 7.58 us -> 3.52 us  [per_device(): lax.all_to_all(blocks, 'grp', 0, 0, tiled=True)]
    all_to_all x1, blocking collectives: 11.9 us -> 13.8 us  [per_device(): lax.all_to_all(jnp.broadcast_to(tile_src, (n_grp, n_tiles)), 'grp', 0, 0,...]
    pallas_call x1, Pallas kernels: 3.45 us -> 2.16 us  [per_device(): pl.pallas_call(remote_kernel, name='remote', out_shape=jax.ShapeDtypeStru...]
    pallas_call x1, Pallas kernels: 1.4 us -> 2.06 us  [per_device(): pl.pallas_call(gather_kernel, name='gather', out_shape=jax.ShapeDtypeStru...]
    broadcast_in_dim x1, local copies, waits for them, and re-layouts: 1.3 us -> 0.69 us  [per_device(): jnp.broadcast_to(tile_src, (n_grp, n_tiles))]
    all_to_all x1, blocking collectives: 18.3 us -> 18.9 us  [per_device(): rows = lax.all_to_all(aggregated, 'col', 0, 0, tiled=True).reshape(-1, 128)]
where the time goes in v3:
time: 49.5 us; the launch traced here: 48.7 us
  blocking collectives  32.7 us (66%)
  Pallas kernels  9.26 us (19%)
  starting transfers between devices  3.52 us (7%)
  waiting for transfers between devices  1.62 us (3%)
  matrix products  0.8 us (2%)
  local copies, waits for them, and re-layouts  0.71 us (1%)
    all_to_all x1, blocking collectives, per_device(): rows = lax.all_to_all(aggregated, 'col', 0, 0, tiled=True).reshape(-1, 128)  18.9 us
    all_to_all x1, blocking collectives, per_device(): lax.all_to_all(jnp.broadcast_to(tile_src, (n_grp, n_tiles)), 'grp', 0, 0,...  13.8 us
    pallas_call x1, Pallas kernels, per_device(): pl.pallas_call(local_kernel, name='local', out_shape=(pltpu.VMEM((n_dst +...  5.05 us
    all_to_all x1, starting transfers between devices, per_device(): lax.all_to_all(blocks, 'grp', 0, 0, tiled=True)  3.52 us
    pallas_call x1, Pallas kernels, per_device(): pl.pallas_call(remote_kernel, name='remote', out_shape=jax.ShapeDtypeStru...  2.16 us
    pallas_call x1, Pallas kernels, per_device(): pl.pallas_call(gather_kernel, name='gather', out_shape=jax.ShapeDtypeStru...  2.06 us
    all_to_all x1, waiting for transfers between devices, per_device(): lax.all_to_all(blocks, 'grp', 0, 0, tiled=True)  1.62 us
  transfers between devices with their start and end apart: 1, of which 1 were waited for; matrix products, arithmetic and copies ran while one was open for 0% of the time, Pallas kernels for 10%

profile of v3, /device:TPU:1, one launch (start us, length us, event | category | flops | bytes accessed | tf_op | source)
XLA Modules:
  0.0 48.7 jit_solution(14367435968634524253)
XLA Ops:
  0.0 0.0 copy-start
  0.0 0.7 %broadcast_in_dim.4 = s32[16,1,256]{2,1,0:T(1,128)S(1)} broadcast(s32[256]{0:T(256)} %param.11), dimensions={2} | broadcast | bytes 17408 | tf_op jit(solution)/shard_map/broadcast_in_dim | solution.py:238
  0.7 13.8 %all_to_all.18 = s32[16,1,256]{2,1,0:T(1,128)S(1)} all-to-all(s32[16,1,256]{2,1,0:T(1,128)S(1)} %broadcast_in_dim.4), channel_id=1, replica_groups=mesh['grp'=16,'col'=16] {'grp'}, dimensions={0} | all-to-all | bytes 32768 | tf_op jit(solution)/shard_map/all_to_all | solution.py:237
  14.5 2.1 %gather.1 = bf16[16,4,8,128]{3,2,1,0:T(8,128)(2,1)} custom-call(s32[16,256]{1,0:T(8,128)S(1)} %bitcast.12, bf16[8,65536]{1,0:T(8,128)(2,1)} %feat_h.3), custom_call_target="tpu_custom_call" | custom-call | tf_op jit(solution)/shard_map/gather/pallas_call | solution.py:276
  16.6 3.5 %all-to-all-start.1 = ((bf16[16,4,8,128]{3,2,1,0:T(8,128)(2,1)}), bf16[16,4,8,128]{3,2,1,0:T(8,128)(2,1)S(1)}, u32[]{:S(2)}, u32[]{:S(2)}) async-start(bf16[16,4,8,128]{3,2,1,0:T(8,128)(2,1)} %gather.1), calls=%async_computation.1 | async-start | bytes 262144 | tf_op jit(solution)/shard_map/all_to_all | solution.py:290
  20.1 0.0 copy-start.1
  20.1 5.0 %local.1 = (f32[17,8,128]{2,1,0:T(8,128)S(1)}, bf16[96,128,128]{2,1,0:T(8,128)(2,1)S(1)}, s32[297]{0:T(512)S(4)}) custom-call(s32[1,256]{1,0:T(1,128)} %bitcast.14, s32[1,256]{1,0:T(1,128)} %bitcast.15, s32[16]{0:T(128)} %ids_h.1, f32[16,128]{1,0:T(8,128)} %bitcast.13, bf16[8,65536]{1,0:T(8,128)(2,1)} %feat_h.3, bf16[256,128,128]{2,1,0:T(8,128)(2,1)} %adj_h.3), custom_call_target="tpu_custom_call" | custom-call | flops 268435456 | bytes 18874368 | tf_op jit(solution)/shard_map/local/pallas_call | solution.py:240
  25.2 1.6 %all-to-all-done.1 = bf16[16,4,8,128]{3,2,1,0:T(8,128)(2,1)S(1)} async-done(((bf16[16,4,8,128]{3,2,1,0:T(8,128)(2,1)}), bf16[16,4,8,128]{3,2,1,0:T(8,128)(2,1)S(1)}, u32[]{:S(2)}, u32[]{:S(2)}) %all-to-all-start.1) | async-done | bytes 131104 | tf_op jit(solution)/shard_map/all_to_all | solution.py:290
  26.8 2.2 %remote.1 = bf16[16,8,128]{2,1,0:T(8,128)(2,1)S(1)} custom-call(s32[297]{0:T(512)S(4)} %get-tuple-element.8.remote_s, bf16[64,8,128]{2,1,0:T(8,128)(2,1)S(1)} %bitcast.11, f32[17,8,128]{2,1,0:T(8,128)S(1)} %get-tuple-element.9.acc_in_ref, bf16[96,128,128]{2,1,0:T(8,128)(2,1)S(1)} %get-tuple-element.10.held_ref, bf16[256,128,128]{2,1,0:T(8,128)(2,1)} %adj_h.3), custom_call_target="tpu_custom_call" | custom-call | tf_op jit(solution)/shard_map/remote/pallas_call | solution.py:291
  29.0 18.9 %all_to_all.19 = bf16[16,8,128]{2,1,0:T(8,128)(2,1)S(1)} all-to-all(bf16[16,8,128]{2,1,0:T(8,128)(2,1)S(1)} %remote.1), channel_id=1, replica_groups=mesh['grp'=16,'col'=16] {'col'}, dimensions={0} | all-to-all | bytes 65536 | tf_op jit(solution)/shard_map/all_to_all | solution.py:308
  47.8 0.0 copy-done
  47.8 0.0 copy-done.1
  47.8 0.8 %fusion.1 = bf16[128,128]{1,0:T(8,128)(2,1)} fusion(bf16[128,128]{1,0:T(8,128)(2,1)S(1)} %copy-done, bf16[16,8,128]{2,1,0:T(8,128)(2,1)S(1)} %all_to_all.19, f32[128]{0:T(128)S(1)} %copy-done.1), kind=kOutput, calls=%fused_computation.2 | convolution fusion | flops 4243456 | bytes 98816 | tf_op jit(solution)/shard_map/dot_general | solution.py:310
  (1 shorter events, 0.0 us)
Async XLA Ops:
  0.0 47.8 %copy-start = (bf16[128,128]{1,0:T(8,128)(2,1)S(1)}, bf16[128,128]{1,0:T(8,128)(2,1)}, u32[]{:S(2)}) copy-start(bf16[128,128]{1,0:T(8,128)(2,1)} %param.14) | copy-start | bytes 98308
  16.6 10.2 %all-to-all-start.1 = ((bf16[16,4,8,128]{3,2,1,0:T(8,128)(2,1)}), bf16[16,4,8,128]{3,2,1,0:T(8,128)(2,1)S(1)}, u32[]{:S(2)}, u32[]{:S(2)}) async-start(bf16[16,4,8,128]{3,2,1,0:T(8,128)(2,1)} %gather.1), calls=%async_computation.1 | async-start | bytes 262144 | tf_op jit(solution)/shard_map/all_to_all | solution.py:290
  20.1 27.7 %copy-start.1 = (f32[128]{0:T(128)S(1)}, f32[128]{0:T(128)}, u32[]{:S(2)}) copy-start(f32[128]{0:T(128)} %param.15) | copy-start | bytes 1540

commit v4 on v3

--- a/solution.py
+++ b/solution.py
@@ -8,6 +8,7 @@
 NEED = 4
 BATCH = 32
 HELD = 96
+LATE = 40
 FETCH = 8
 PAD = 40
 CHUNK = 16
@@ -22,11 +23,12 @@
 
 
 def four_least(values):
+    values = values.astype(jnp.float32)
     least = []
     for _ in range(NEED):
         low = jnp.min(values, axis=1, keepdims=True)
-        least.append(low)
-        values = jnp.where(values > low, values, BIG)
+        least.append(low.astype(jnp.int32))
+        values = jnp.where(values > low, values, float(BIG))
     return least
 
 
@@ -138,7 +140,7 @@
     n_remote = n_tiles - n_local
     for i in range(PAD):
         local_s[n_local + i] = n_dst * 256 + n_tiles - 1
-        remote_s[n_remote + i] = n_dst * 256 + n_tiles - 1
+        remote_s[n_remote + i] = n_dst * 256 + n_tiles - PAD + i
     remote_s[remote_s.shape[0] - 1] = n_remote
     copies[2].wait()
     copies[3].wait()
@@ -164,27 +166,29 @@
     lax.fori_loop(0, HELD, hold, 0, unroll=8)
 
 
-def gather_kernel(req_ref, feat_h, out_ref, feat_ref, place_v, place_s, sems):
-    fetch = pltpu.make_async_copy(feat_h, feat_ref, sems.at[0])
+def spread_kernel(src_h, feat_h, out_ref, feat_ref, src_v, sems):
+    copy = pltpu.make_async_copy(src_h, src_v, sems.at[0])
+    copy.start()
+    fetch = pltpu.make_async_copy(feat_h, feat_ref, sems.at[1])
     fetch.start()
+    copy.wait()
+    out_ref[...] = jnp.broadcast_to(src_v[...][None], out_ref.shape)
+    fetch.wait()
+
+
+def gather_kernel(req_ref, feat_ref, out_ref):
     group = lax.axis_index("grp")
     group_len = feat_ref.shape[1] // 128
     shift = group_len.bit_length() - 1
-    n_grp, n_tiles = req_ref.shape
     req = req_ref[...]
     least = four_least(jnp.where((req >> shift) == group, req & (group_len - 1), BIG))
-    lane = lax.broadcasted_iota(jnp.int32, (n_grp, 128), 1)
-    table = jnp.zeros((n_grp, 128), jnp.int32)
+    lane = lax.broadcasted_iota(jnp.int32, (req.shape[0], 128), 1)
+    table = jnp.zeros((req.shape[0], 128), jnp.int32)
     for r, low in enumerate(least):
         table = jnp.where(lane == r, jnp.minimum(low, group_len - 1), table)
-    place_v[...] = table
-    copy = pltpu.make_async_copy(place_v, place_s, sems.at[1])
-    copy.start()
-    copy.wait()
-    fetch.wait()
-    for k in range(n_grp):
+    for k in range(req.shape[0]):
         for r in range(NEED):
-            place = pl.multiple_of(place_s[k, r] * 128, 128)
+            place = pl.multiple_of(table[k, r] * 128, 128)
             out_ref[k, r] = feat_ref[:, pl.ds(place, 128)]
 
 
@@ -193,37 +197,38 @@
 ):
     n_remote = remote_s[remote_s.shape[0] - 1]
 
-    def fetch(i, sem):
-        pltpu.make_async_copy(adj_h.at[remote_s[i] & 255], adj_ref.at[i - HELD], sem).start()
-
-    def arrive(first, count, sem):
-        tiles = pl.ds(first - HELD, count)
-        pltpu.make_async_copy(adj_h.at[pl.ds(0, count)], adj_ref.at[tiles], sem).wait()
+    n_passes = (jnp.maximum(n_remote - HELD, 0) + LATE - 1) // LATE
+
+    def fetch_some(i, step):
+        for q in range(FETCH):
+            place = step * LATE + i * FETCH + q
+            pltpu.make_async_copy(
+                adj_h.at[remote_s[HELD + place] & 255], adj_ref.at[place], sems.at[step]
+            ).start()
+        return step
 
     def fetch_pass(step, carry):
-        def some(i, c):
-            for q in range(FETCH):
-                fetch(step * BATCH + i * FETCH + q, sems.at[step])
-            return c
-
-        return lax.fori_loop(0, BATCH // FETCH, some, carry)
-
-    n_passes = (n_remote + BATCH - 1) // BATCH
-    lax.fori_loop(HELD // BATCH, n_passes, fetch_pass, 0)
+        lax.fori_loop(0, LATE // FETCH, fetch_some, step)
+        return carry
+
+    lax.fori_loop(0, n_passes, fetch_pass, 0)
     acc_ref[...] = acc_in_ref[...]
 
     def load_x(slot):
         return recv_ref[slot].astype(jnp.float32)
 
     def late_pass(step, carry):
-        arrive(pl.multiple_of(step * BATCH, BATCH), BATCH, sems.at[step])
+        first = pl.multiple_of(step * LATE, LATE)
+        pltpu.make_async_copy(
+            adj_h.at[pl.ds(0, LATE)], adj_ref.at[pl.ds(first, LATE)], sems.at[step]
+        ).wait()
         tile_pass(
-            remote_s, step * BATCH, BATCH, load_x, lambda index, _: adj_ref[index - HELD], acc_ref
+            remote_s, HELD + first, LATE, load_x, lambda index, _: adj_ref[index - HELD], acc_ref
         )
         return carry
 
     tile_pass(remote_s, 0, HELD, load_x, lambda index, _: held_ref[index], acc_ref)
-    lax.fori_loop(HELD // BATCH, n_passes, late_pass, 0)
+    lax.fori_loop(0, n_passes, late_pass, 0)
     out_ref[...] = acc_ref[: out_ref.shape[0]].astype(out_ref.dtype)
 
 
@@ -234,9 +239,22 @@
     n_grp = lax.axis_size("grp")
     n_slots = n_grp * NEED
     params = pltpu.CompilerParams(vmem_limit_bytes=16 << 20)
-    requests = lax.all_to_all(
-        jnp.broadcast_to(tile_src, (n_grp, n_tiles)), "grp", 0, 0, tiled=True
-    )
+    spread, feat_held = pl.pallas_call(
+        spread_kernel,
+        name="spread",
+        out_shape=(
+            pltpu.VMEM((n_grp, 1, n_tiles), jnp.int32),
+            pltpu.VMEM(features.shape, features.dtype),
+        ),
+        in_specs=[HBM, HBM],
+        out_specs=(VMEM, VMEM),
+        scratch_shapes=[pltpu.VMEM((1, n_tiles), jnp.int32), pltpu.SemaphoreType.DMA((2,))],
+        compiler_params=pltpu.CompilerParams(vmem_limit_bytes=4 << 20),
+    )(
+        pltpu.with_memory_space_constraint(tile_src.reshape(1, n_tiles), pltpu.HBM),
+        pltpu.with_memory_space_constraint(features, pltpu.HBM),
+    )
+    requests = lax.all_to_all(spread, "grp", 0, 0, tiled=True).reshape(n_grp, n_tiles)
     acc, adj_held, remote = pl.pallas_call(
         local_kernel,
         name="local",
@@ -277,16 +295,10 @@
         gather_kernel,
         name="gather",
         out_shape=jax.ShapeDtypeStruct((n_grp, NEED, n_feat, 128), features.dtype),
-        in_specs=[VMEM, HBM],
+        in_specs=[VMEM, VMEM],
         out_specs=VMEM,
-        scratch_shapes=[
-            pltpu.VMEM(features.shape, features.dtype),
-            pltpu.VMEM((n_grp, 128), jnp.int32),
-            pltpu.SMEM((n_grp, 128), jnp.int32),
-            pltpu.SemaphoreType.DMA((2,)),
-        ],
-        compiler_params=params,
-    )(requests, pltpu.with_memory_space_constraint(features, pltpu.HBM))
+        compiler_params=pltpu.CompilerParams(vmem_limit_bytes=4 << 20),
+    )(requests, pltpu.with_memory_space_constraint(feat_held, pltpu.VMEM))
     arrived = lax.all_to_all(blocks, "grp", 0, 0, tiled=True).reshape(n_slots, n_feat, 128)
     aggregated = pl.pallas_call(
         remote_kernel,
@@ -297,7 +309,7 @@
         scratch_shapes=[
             pltpu.VMEM((n_tiles - HELD,) + adj_tiles.shape[1:], adj_tiles.dtype),
             pltpu.VMEM((n_dst + 1, n_feat, 128), jnp.float32),
-            pltpu.SemaphoreType.DMA((n_tiles // BATCH,)),
+            pltpu.SemaphoreType.DMA(((n_tiles - HELD) // LATE,)),
         ],
         compiler_params=params,
     )(

time: 49.5 us -> 48.8 us (0.986)
  local copies, waits for them, and re-layouts: 0.71 us -> 0.01 us
    pallas_call x0 -> x1, Pallas kernels: none -> 1.26 us  [per_device(): pl.pallas_call(spread_kernel, name='spread', out_shape=(pltpu.VMEM((n_grp...]
    pallas_call x1, Pallas kernels: 2.06 us -> 1.15 us  [per_device(): pl.pallas_call(gather_kernel, name='gather', out_shape=jax.ShapeDtypeStru...]
    broadcast_in_dim x1 -> x0, local copies, waits for them, and re-layouts: 0.69 us -> none  [per_device(): jnp.broadcast_to(tile_src, (n_grp, n_tiles))]
where the time goes in v4:
time: 48.8 us; the launch traced here: 48.4 us
  blocking collectives  32.7 us (67%)
  Pallas kernels  9.43 us (19%)
  starting transfers between devices  3.51 us (7%)
  waiting for transfers between devices  1.89 us (4%)
  matrix products  0.8 us (2%)
    all_to_all x1, blocking collectives, per_device(): rows = lax.all_to_all(aggregated, 'col', 0, 0, tiled=True).reshape(-1, 128)  18.9 us
    all_to_all x1, blocking collectives, per_device(): lax.all_to_all(spread, 'grp', 0, 0, tiled=True).reshape(n_grp, n_tiles)  13.8 us
    pallas_call x1, Pallas kernels, per_device(): pl.pallas_call(local_kernel, name='local', out_shape=(pltpu.VMEM((n_dst +...  4.78 us
    all_to_all x1, starting transfers between devices, per_device(): lax.all_to_all(blocks, 'grp', 0, 0, tiled=True)  3.51 us
    pallas_call x1, Pallas kernels, per_device(): pl.pallas_call(remote_kernel, name='remote', out_shape=jax.ShapeDtypeStru...  2.24 us
    all_to_all x1, waiting for transfers between devices, per_device(): lax.all_to_all(blocks, 'grp', 0, 0, tiled=True)  1.89 us
    pallas_call x1, Pallas kernels, per_device(): pl.pallas_call(spread_kernel, name='spread', out_shape=(pltpu.VMEM((n_grp...  1.26 us
    pallas_call x1, Pallas kernels, per_device(): pl.pallas_call(gather_kernel, name='gather', out_shape=jax.ShapeDtypeStru...  1.15 us
  transfers between devices with their start and end apart: 1, of which 1 were waited for; matrix products, arithmetic and copies ran while one was open for 0% of the time, Pallas kernels for 10%

profile of v4, /device:TPU:1, one launch (start us, length us, event | category | flops | bytes accessed | tf_op | source)
XLA Modules:
  0.0 48.4 jit_solution(13179518682273123761)
XLA Ops:
  0.0 0.0 copy-start
  0.0 1.3 %spread.1 = (s32[16,1,256]{2,1,0:T(1,128)S(1)}, bf16[8,65536]{1,0:T(8,128)(2,1)S(1)}) custom-call(s32[1,256]{1,0:T(1,128)} %bitcast.14, bf16[8,65536]{1,0:T(8,128)(2,1)} %feat_h.3), custom_call_target="tpu_custom_call" | custom-call | tf_op jit(solution)/shard_map/spread/pallas_call | solution.py:242
  1.3 13.8 %all_to_all.15 = s32[16,1,256]{2,1,0:T(1,128)S(1)} all-to-all(s32[16,1,256]{2,1,0:T(1,128)S(1)} %get-tuple-element.11), channel_id=1, replica_groups=mesh['grp'=16,'col'=16] {'grp'}, dimensions={0} | all-to-all | bytes 32768 | tf_op jit(solution)/shard_map/all_to_all | solution.py:257
  15.1 1.1 %gather.1 = bf16[16,4,8,128]{3,2,1,0:T(8,128)(2,1)} custom-call(s32[16,256]{1,0:T(8,128)S(1)} %bitcast.12, bf16[8,65536]{1,0:T(8,128)(2,1)S(1)} %get-tuple-element.12.feat_ref), custom_call_target="tpu_custom_call" | custom-call | tf_op jit(solution)/shard_map/gather/pallas_call | solution.py:294
  16.3 3.5 %all-to-all-start.1 = ((bf16[16,4,8,128]{3,2,1,0:T(8,128)(2,1)}), bf16[16,4,8,128]{3,2,1,0:T(8,128)(2,1)S(1)}, u32[]{:S(2)}, u32[]{:S(2)}) async-start(bf16[16,4,8,128]{3,2,1,0:T(8,128)(2,1)} %gather.1), calls=%async_computation.1 | async-start | bytes 262144 | tf_op jit(solution)/shard_map/all_to_all | solution.py:302
  19.8 0.0 copy-start.1
  19.8 4.8 %local.1 = (f32[17,8,128]{2,1,0:T(8,128)S(1)}, bf16[96,128,128]{2,1,0:T(8,128)(2,1)S(1)}, s32[297]{0:T(512)S(4)}) custom-call(s32[1,256]{1,0:T(1,128)} %bitcast.15, s32[1,256]{1,0:T(1,128)} %bitcast.16, s32[16]{0:T(128)} %ids_h.1, f32[16,128]{1,0:T(8,128)} %bitcast.13, bf16[8,65536]{1,0:T(8,128)(2,1)} %feat_h.3, bf16[256,128,128]{2,1,0:T(8,128)(2,1)} %adj_h.3), custom_call_target="tpu_custom_call" | custom-call | flops 268435456 | bytes 18874368 | tf_op jit(solution)/shard_map/local/pallas_call | solution.py:258
  24.6 1.9 %all-to-all-done.1 = bf16[16,4,8,128]{3,2,1,0:T(8,128)(2,1)S(1)} async-done(((bf16[16,4,8,128]{3,2,1,0:T(8,128)(2,1)}), bf16[16,4,8,128]{3,2,1,0:T(8,128)(2,1)S(1)}, u32[]{:S(2)}, u32[]{:S(2)}) %all-to-all-start.1) | async-done | bytes 131104 | tf_op jit(solution)/shard_map/all_to_all | solution.py:302
  26.5 2.2 %remote.1 = bf16[16,8,128]{2,1,0:T(8,128)(2,1)S(1)} custom-call(s32[297]{0:T(512)S(4)} %get-tuple-element.10.remote_s, bf16[64,8,128]{2,1,0:T(8,128)(2,1)S(1)} %bitcast.11, f32[17,8,128]{2,1,0:T(8,128)S(1)} %get-tuple-element.13.acc_in_ref, bf16[96,128,128]{2,1,0:T(8,128)(2,1)S(1)} %get-tuple-element.14.held_ref, bf16[256,128,128]{2,1,0:T(8,128)(2,1)} %adj_h.3), custom_call_target="tpu_custom_call" | custom-call | tf_op jit(solution)/shard_map/remote/pallas_call | solution.py:303
  28.7 18.9 %all_to_all.16 = bf16[16,8,128]{2,1,0:T(8,128)(2,1)S(1)} all-to-all(bf16[16,8,128]{2,1,0:T(8,128)(2,1)S(1)} %remote.1), channel_id=1, replica_groups=mesh['grp'=16,'col'=16] {'col'}, dimensions={0} | all-to-all | bytes 65536 | tf_op jit(solution)/shard_map/all_to_all | solution.py:320
  47.6 0.0 copy-done
  47.6 0.0 copy-done.1
  47.6 0.8 %fusion.1 = bf16[128,128]{1,0:T(8,128)(2,1)} fusion(bf16[128,128]{1,0:T(8,128)(2,1)S(1)} %copy-done, bf16[16,8,128]{2,1,0:T(8,128)(2,1)S(1)} %all_to_all.16, f32[128]{0:T(128)S(1)} %copy-done.1), kind=kOutput, calls=%fused_computation.2 | convolution fusion | flops 4243456 | bytes 98816 | tf_op jit(solution)/shard_map/dot_general | solution.py:322
  (1 shorter events, 0.0 us)
Async XLA Ops:
  0.0 47.6 %copy-start = (bf16[128,128]{1,0:T(8,128)(2,1)S(1)}, bf16[128,128]{1,0:T(8,128)(2,1)}, u32[]{:S(2)}) copy-start(bf16[128,128]{1,0:T(8,128)(2,1)} %param.14) | copy-start | bytes 98308
  16.3 10.2 %all-to-all-start.1 = ((bf16[16,4,8,128]{3,2,1,0:T(8,128)(2,1)}), bf16[16,4,8,128]{3,2,1,0:T(8,128)(2,1)S(1)}, u32[]{:S(2)}, u32[]{:S(2)}) async-start(bf16[16,4,8,128]{3,2,1,0:T(8,128)(2,1)} %gather.1), calls=%async_computation.1 | async-start | bytes 262144 | tf_op jit(solution)/shard_map/all_to_all | solution.py:302
  19.8 27.8 %copy-start.1 = (f32[128]{0:T(128)S(1)}, f32[128]{0:T(128)}, u32[]{:S(2)}) copy-start(f32[128]{0:T(128)} %param.15) | copy-start | bytes 1540

commit v5 on v4

--- a/solution.py
+++ b/solution.py
@@ -7,9 +7,9 @@
 
 NEED = 4
 BATCH = 32
-HELD = 96
-LATE = 40
-FETCH = 8
+HELD = 100
+LATE = 36
+FETCH = 12
 PAD = 40
 CHUNK = 16
 EARLY = 2
@@ -307,9 +307,9 @@
         in_specs=[SMEM, VMEM, VMEM, VMEM, HBM],
         out_specs=VMEM,
         scratch_shapes=[
-            pltpu.VMEM((n_tiles - HELD,) + adj_tiles.shape[1:], adj_tiles.dtype),
+            pltpu.VMEM((-(-(n_tiles - HELD) // LATE) * LATE,) + adj_tiles.shape[1:], adj_tiles.dtype),
             pltpu.VMEM((n_dst + 1, n_feat, 128), jnp.float32),
-            pltpu.SemaphoreType.DMA(((n_tiles - HELD) // LATE,)),
+            pltpu.SemaphoreType.DMA((-(-(n_tiles - HELD) // LATE),)),
         ],
         compiler_params=params,
     )(

time: 48.8 us -> 48.6 us (level)
  transfers between devices with their start and end apart: 1 -> 1, of which waited for: 1 -> 1; matrix products, arithmetic and copies ran while one was open for 0% -> 0% of each run, Pallas kernels for 10% -> 11%
where the time goes in v5:
time: 48.6 us; the launch traced here: 48.3 us
  blocking collectives  32.7 us (67%)
  Pallas kernels  9.65 us (20%)
  starting transfers between devices  3.51 us (7%)
  waiting for transfers between devices  1.57 us (3%)
  matrix products  0.8 us (2%)
    all_to_all x1, blocking collectives, per_device(): rows = lax.all_to_all(aggregated, 'col', 0, 0, tiled=True).reshape(-1, 128)  18.9 us
    all_to_all x1, blocking collectives, per_device(): lax.all_to_all(spread, 'grp', 0, 0, tiled=True).reshape(n_grp, n_tiles)  13.8 us
    pallas_call x1, Pallas kernels, per_device(): pl.pallas_call(local_kernel, name='local', out_shape=(pltpu.VMEM((n_dst +...  5.1 us
    all_to_all x1, starting transfers between devices, per_device(): lax.all_to_all(blocks, 'grp', 0, 0, tiled=True)  3.51 us
    pallas_call x1, Pallas kernels, per_device(): pl.pallas_call(remote_kernel, name='remote', out_shape=jax.ShapeDtypeStru...  2.14 us
    all_to_all x1, waiting for transfers between devices, per_device(): lax.all_to_all(blocks, 'grp', 0, 0, tiled=True)  1.57 us
    pallas_call x1, Pallas kernels, per_device(): pl.pallas_call(spread_kernel, name='spread', out_shape=(pltpu.VMEM((n_grp...  1.26 us
    pallas_call x1, Pallas kernels, per_device(): pl.pallas_call(gather_kernel, name='gather', out_shape=jax.ShapeDtypeStru...  1.15 us
  transfers between devices with their start and end apart: 1, of which 1 were waited for; matrix products, arithmetic and copies ran while one was open for 0% of the time, Pallas kernels for 11%

profile of v5, /device:TPU:1, one launch (start us, length us, event | category | flops | bytes accessed | tf_op | source)
XLA Modules:
  0.0 48.3 jit_solution(3627290937045314079)
XLA Ops:
  0.0 0.0 copy-start
  0.0 1.3 %spread.1 = (s32[16,1,256]{2,1,0:T(1,128)S(1)}, bf16[8,65536]{1,0:T(8,128)(2,1)S(1)}) custom-call(s32[1,256]{1,0:T(1,128)} %bitcast.14, bf16[8,65536]{1,0:T(8,128)(2,1)} %feat_h.3), custom_call_target="tpu_custom_call" | custom-call | tf_op jit(solution)/shard_map/spread/pallas_call | solution.py:242
  1.3 13.8 %all_to_all.15 = s32[16,1,256]{2,1,0:T(1,128)S(1)} all-to-all(s32[16,1,256]{2,1,0:T(1,128)S(1)} %get-tuple-element.11), channel_id=1, replica_groups=mesh['grp'=16,'col'=16] {'grp'}, dimensions={0} | all-to-all | bytes 32768 | tf_op jit(solution)/shard_map/all_to_all | solution.py:257
  15.1 1.1 %gather.1 = bf16[16,4,8,128]{3,2,1,0:T(8,128)(2,1)} custom-call(s32[16,256]{1,0:T(8,128)S(1)} %bitcast.12, bf16[8,65536]{1,0:T(8,128)(2,1)S(1)} %get-tuple-element.12.feat_ref), custom_call_target="tpu_custom_call" | custom-call | tf_op jit(solution)/shard_map/gather/pallas_call | solution.py:294
  16.3 3.5 %all-to-all-start.1 = ((bf16[16,4,8,128]{3,2,1,0:T(8,128)(2,1)}), bf16[16,4,8,128]{3,2,1,0:T(8,128)(2,1)S(1)}, u32[]{:S(2)}, u32[]{:S(2)}) async-start(bf16[16,4,8,128]{3,2,1,0:T(8,128)(2,1)} %gather.1), calls=%async_computation.1 | async-start | bytes 262144 | tf_op jit(solution)/shard_map/all_to_all | solution.py:302
  19.8 0.0 copy-start.1
  19.8 5.1 %local.1 = (f32[17,8,128]{2,1,0:T(8,128)S(1)}, bf16[100,128,128]{2,1,0:T(8,128)(2,1)S(1)}, s32[297]{0:T(512)S(4)}) custom-call(s32[1,256]{1,0:T(1,128)} %bitcast.15, s32[1,256]{1,0:T(1,128)} %bitcast.16, s32[16]{0:T(128)} %ids_h.1, f32[16,128]{1,0:T(8,128)} %bitcast.13, bf16[8,65536]{1,0:T(8,128)(2,1)} %feat_h.3, bf16[256,128,128]{2,1,0:T(8,128)(2,1)} %adj_h.3), custom_call_target="tpu_custom_call" | custom-call | flops 268435456 | bytes 18874368 | tf_op jit(solution)/shard_map/local/pallas_call | solution.py:258
  24.9 1.6 %all-to-all-done.1 = bf16[16,4,8,128]{3,2,1,0:T(8,128)(2,1)S(1)} async-done(((bf16[16,4,8,128]{3,2,1,0:T(8,128)(2,1)}), bf16[16,4,8,128]{3,2,1,0:T(8,128)(2,1)S(1)}, u32[]{:S(2)}, u32[]{:S(2)}) %all-to-all-start.1) | async-done | bytes 131104 | tf_op jit(solution)/shard_map/all_to_all | solution.py:302
  26.5 2.1 %remote.1 = bf16[16,8,128]{2,1,0:T(8,128)(2,1)S(1)} custom-call(s32[297]{0:T(512)S(4)} %get-tuple-element.10.remote_s, bf16[64,8,128]{2,1,0:T(8,128)(2,1)S(1)} %bitcast.11, f32[17,8,128]{2,1,0:T(8,128)S(1)} %get-tuple-element.13.acc_in_ref, bf16[100,128,128]{2,1,0:T(8,128)(2,1)S(1)} %get-tuple-element.14.held_ref, bf16[256,128,128]{2,1,0:T(8,128)(2,1)} %adj_h.3), custom_call_target="tpu_custom_call" | custom-call | tf_op jit(solution)/shard_map/remote/pallas_call | solution.py:303
  28.6 18.9 %all_to_all.16 = bf16[16,8,128]{2,1,0:T(8,128)(2,1)S(1)} all-to-all(bf16[16,8,128]{2,1,0:T(8,128)(2,1)S(1)} %remote.1), channel_id=1, replica_groups=mesh['grp'=16,'col'=16] {'col'}, dimensions={0} | all-to-all | bytes 65536 | tf_op jit(solution)/shard_map/all_to_all | solution.py:320
  47.5 0.0 copy-done
  47.5 0.0 copy-done.1
  47.5 0.8 %fusion.1 = bf16[128,128]{1,0:T(8,128)(2,1)} fusion(bf16[128,128]{1,0:T(8,128)(2,1)S(1)} %copy-done, bf16[16,8,128]{2,1,0:T(8,128)(2,1)S(1)} %all_to_all.16, f32[128]{0:T(128)S(1)} %copy-done.1), kind=kOutput, calls=%fused_computation.2 | convolution fusion | flops 4243456 | bytes 98816 | tf_op jit(solution)/shard_map/dot_general | solution.py:322
  (1 shorter events, 0.0 us)
Async XLA Ops:
  0.0 47.5 %copy-start = (bf16[128,128]{1,0:T(8,128)(2,1)S(1)}, bf16[128,128]{1,0:T(8,128)(2,1)}, u32[]{:S(2)}) copy-start(bf16[128,128]{1,0:T(8,128)(2,1)} %param.14) | copy-start | bytes 98308
  16.3 10.2 %all-to-all-start.1 = ((bf16[16,4,8,128]{3,2,1,0:T(8,128)(2,1)}), bf16[16,4,8,128]{3,2,1,0:T(8,128)(2,1)S(1)}, u32[]{:S(2)}, u32[]{:S(2)}) async-start(bf16[16,4,8,128]{3,2,1,0:T(8,128)(2,1)} %gather.1), calls=%async_computation.1 | async-start | bytes 262144 | tf_op jit(solution)/shard_map/all_to_all | solution.py:302
  19.8 27.7 %copy-start.1 = (f32[128]{0:T(128)S(1)}, f32[128]{0:T(128)}, u32[]{:S(2)}) copy-start(f32[128]{0:T(128)} %param.15) | copy-start | bytes 1540

commit v6 on v5

--- a/solution.py
+++ b/solution.py
@@ -8,8 +8,8 @@
 NEED = 4
 BATCH = 32
 HELD = 100
-LATE = 36
-FETCH = 12
+LATE = 30
+FETCH = 10
 PAD = 40
 CHUNK = 16
 EARLY = 2

time: 48.6 us -> 48.5 us (level)
  no operation moved by 1% of the time
where the time goes in v6:
time: 48.5 us; the launch traced here: 48.1 us
  blocking collectives  32.7 us (67%)
  Pallas kernels  9.5 us (20%)
  starting transfers between devices  3.51 us (7%)
  waiting for transfers between devices  1.58 us (3%)
  matrix products  0.8 us (2%)
    all_to_all x1, blocking collectives, per_device(): rows = lax.all_to_all(aggregated, 'col', 0, 0, tiled=True).reshape(-1, 128)  18.9 us
    all_to_all x1, blocking collectives, per_device(): lax.all_to_all(spread, 'grp', 0, 0, tiled=True).reshape(n_grp, n_tiles)  13.8 us
    pallas_call x1, Pallas kernels, per_device(): pl.pallas_call(local_kernel, name='local', out_shape=(pltpu.VMEM((n_dst +...  5.09 us
    all_to_all x1, starting transfers between devices, per_device(): lax.all_to_all(blocks, 'grp', 0, 0, tiled=True)  3.51 us
    pallas_call x1, Pallas kernels, per_device(): pl.pallas_call(remote_kernel, name='remote', out_shape=jax.ShapeDtypeStru...  1.99 us
    all_to_all x1, waiting for transfers between devices, per_device(): lax.all_to_all(blocks, 'grp', 0, 0, tiled=True)  1.58 us
    pallas_call x1, Pallas kernels, per_device(): pl.pallas_call(spread_kernel, name='spread', out_shape=(pltpu.VMEM((n_grp...  1.26 us
    pallas_call x1, Pallas kernels, per_device(): pl.pallas_call(gather_kernel, name='gather', out_shape=jax.ShapeDtypeStru...  1.15 us
  transfers between devices with their start and end apart: 1, of which 1 were waited for; matrix products, arithmetic and copies ran while one was open for 0% of the time, Pallas kernels for 11%

profile of v6, /device:TPU:1, one launch (start us, length us, event | category | flops | bytes accessed | tf_op | source)
XLA Modules:
  0.0 48.1 jit_solution(17794531232338236500)
XLA Ops:
  0.0 0.0 copy-start
  0.0 1.3 %spread.1 = (s32[16,1,256]{2,1,0:T(1,128)S(1)}, bf16[8,65536]{1,0:T(8,128)(2,1)S(1)}) custom-call(s32[1,256]{1,0:T(1,128)} %bitcast.14, bf16[8,65536]{1,0:T(8,128)(2,1)} %feat_h.3), custom_call_target="tpu_custom_call" | custom-call | tf_op jit(solution)/shard_map/spread/pallas_call | solution.py:242
  1.3 13.8 %all_to_all.15 = s32[16,1,256]{2,1,0:T(1,128)S(1)} all-to-all(s32[16,1,256]{2,1,0:T(1,128)S(1)} %get-tuple-element.11), channel_id=1, replica_groups=mesh['grp'=16,'col'=16] {'grp'}, dimensions={0} | all-to-all | bytes 32768 | tf_op jit(solution)/shard_map/all_to_all | solution.py:257
  15.1 1.1 %gather.1 = bf16[16,4,8,128]{3,2,1,0:T(8,128)(2,1)} custom-call(s32[16,256]{1,0:T(8,128)S(1)} %bitcast.12, bf16[8,65536]{1,0:T(8,128)(2,1)S(1)} %get-tuple-element.12.feat_ref), custom_call_target="tpu_custom_call" | custom-call | tf_op jit(solution)/shard_map/gather/pallas_call | solution.py:294
  16.3 3.5 %all-to-all-start.1 = ((bf16[16,4,8,128]{3,2,1,0:T(8,128)(2,1)}), bf16[16,4,8,128]{3,2,1,0:T(8,128)(2,1)S(1)}, u32[]{:S(2)}, u32[]{:S(2)}) async-start(bf16[16,4,8,128]{3,2,1,0:T(8,128)(2,1)} %gather.1), calls=%async_computation.1 | async-start | bytes 262144 | tf_op jit(solution)/shard_map/all_to_all | solution.py:302
  19.8 0.0 copy-start.1
  19.8 5.1 %local.1 = (f32[17,8,128]{2,1,0:T(8,128)S(1)}, bf16[100,128,128]{2,1,0:T(8,128)(2,1)S(1)}, s32[297]{0:T(512)S(4)}) custom-call(s32[1,256]{1,0:T(1,128)} %bitcast.15, s32[1,256]{1,0:T(1,128)} %bitcast.16, s32[16]{0:T(128)} %ids_h.1, f32[16,128]{1,0:T(8,128)} %bitcast.13, bf16[8,65536]{1,0:T(8,128)(2,1)} %feat_h.3, bf16[256,128,128]{2,1,0:T(8,128)(2,1)} %adj_h.3), custom_call_target="tpu_custom_call" | custom-call | flops 268435456 | bytes 18874368 | tf_op jit(solution)/shard_map/local/pallas_call | solution.py:258
  24.9 1.6 %all-to-all-done.1 = bf16[16,4,8,128]{3,2,1,0:T(8,128)(2,1)S(1)} async-done(((bf16[16,4,8,128]{3,2,1,0:T(8,128)(2,1)}), bf16[16,4,8,128]{3,2,1,0:T(8,128)(2,1)S(1)}, u32[]{:S(2)}, u32[]{:S(2)}) %all-to-all-start.1) | async-done | bytes 131104 | tf_op jit(solution)/shard_map/all_to_all | solution.py:302
  26.5 2.0 %remote.1 = bf16[16,8,128]{2,1,0:T(8,128)(2,1)S(1)} custom-call(s32[297]{0:T(512)S(4)} %get-tuple-element.10.remote_s, bf16[64,8,128]{2,1,0:T(8,128)(2,1)S(1)} %bitcast.11, f32[17,8,128]{2,1,0:T(8,128)S(1)} %get-tuple-element.13.acc_in_ref, bf16[100,128,128]{2,1,0:T(8,128)(2,1)S(1)} %get-tuple-element.14.held_ref, bf16[256,128,128]{2,1,0:T(8,128)(2,1)} %adj_h.3), custom_call_target="tpu_custom_call" | custom-call | tf_op jit(solution)/shard_map/remote/pallas_call | solution.py:303
  28.5 18.9 %all_to_all.16 = bf16[16,8,128]{2,1,0:T(8,128)(2,1)S(1)} all-to-all(bf16[16,8,128]{2,1,0:T(8,128)(2,1)S(1)} %remote.1), channel_id=1, replica_groups=mesh['grp'=16,'col'=16] {'col'}, dimensions={0} | all-to-all | bytes 65536 | tf_op jit(solution)/shard_map/all_to_all | solution.py:320
  47.3 0.0 copy-done
  47.3 0.0 copy-done.1
  47.3 0.8 %fusion.1 = bf16[128,128]{1,0:T(8,128)(2,1)} fusion(bf16[128,128]{1,0:T(8,128)(2,1)S(1)} %copy-done, bf16[16,8,128]{2,1,0:T(8,128)(2,1)S(1)} %all_to_all.16, f32[128]{0:T(128)S(1)} %copy-done.1), kind=kOutput, calls=%fused_computation.2 | convolution fusion | flops 4243456 | bytes 98816 | tf_op jit(solution)/shard_map/dot_general | solution.py:322
  (1 shorter events, 0.0 us)
Async XLA Ops:
  0.0 47.3 %copy-start = (bf16[128,128]{1,0:T(8,128)(2,1)S(1)}, bf16[128,128]{1,0:T(8,128)(2,1)}, u32[]{:S(2)}) copy-start(bf16[128,128]{1,0:T(8,128)(2,1)} %param.14) | copy-start | bytes 98308
  16.3 10.2 %all-to-all-start.1 = ((bf16[16,4,8,128]{3,2,1,0:T(8,128)(2,1)}), bf16[16,4,8,128]{3,2,1,0:T(8,128)(2,1)S(1)}, u32[]{:S(2)}, u32[]{:S(2)}) async-start(bf16[16,4,8,128]{3,2,1,0:T(8,128)(2,1)} %gather.1), calls=%async_computation.1 | async-start | bytes 262144 | tf_op jit(solution)/shard_map/all_to_all | solution.py:302
  19.8 27.5 %copy-start.1 = (f32[128]{0:T(128)S(1)}, f32[128]{0:T(128)}, u32[]{:S(2)}) copy-start(f32[128]{0:T(128)} %param.15) | copy-start | bytes 1540
